TPU v7x, 128 devices: a whole 4x4x4 slice. The times are simulated.
128 devices in a mesh: row: 16 (over x_lo, z, core), col: 8 (over y, x_hi).
Axes of the slice: x: 4 (x_hi: 2, x_lo: 2; x = x_hi * 2 + x_lo), y: 4, z: 4, core: 2. Of those that a mesh axis runs over, the one named last changes fastest.
Arguments:
- features: bfloat16 [16384, 768], P(('col', 'row')), may hold values from -6 to 6
- w_neigh: bfloat16 [768, 1024], replicated, may hold values from -0.875 to 0.875
- w_self: bfloat16 [768, 1024], replicated, may hold values from -0.21875 to 0.21875
- bias: float32 [1024], replicated, may hold values from -3 to 3
- cotangent: bfloat16 [16384, 1024], P(('row', 'col')), may hold values from -6 to 6
- block_rows: int32 [16, 8, 96], P('row', 'col'), may hold values from 0 to 7
- block_cols: int32 [16, 8, 96], P('row', 'col'), may hold values from 0 to 15
- block_vals: bfloat16 [16, 8, 96, 128, 128], P('row', 'col'), may hold values from 0 to 1, as said below
- block_count: int32 [16, 8], P('row', 'col'), may hold values from 24 to 96, as said below
Outputs:
- output: bfloat16 [16384, 1024], P(('row', 'col'))
- grad_input: bfloat16 [16384, 768], P(('col', 'row'))
- grad_self: float32 [768, 1024], replicated
- grad_neigh: float32 [768, 1024], replicated
- grad_bias: float32 [1024], replicated
Inputs may be any that keep to these rules, and one draw needn't show every extreme that they name: `block_vals`: block values are non-negative edge weights. `block_count`: some tile in every draw has all 96 slots live.
All inputs are finite; a program needn't handle non-finite values.
Results may differ from a plain program's by a relative error of at most 0.0053.
Values may be sent and summed in bfloat16 or wider, within the bound.
A program may use at most 128 MiB of HBM per device.

v0:
```python
import math

import jax
import jax.numpy as jnp
from jax import lax
from jax.sharding import PartitionSpec as P


def block_term(
    block_vals, take_ids, put_ids, live_count, source, seg_count, flipped, start_slot, group_size
):
    chosen = lax.dynamic_slice_in_dim(block_vals, start_slot, group_size, 0)
    taken = lax.dynamic_slice_in_dim(take_ids, start_slot, group_size, 0)
    placed = lax.dynamic_slice_in_dim(put_ids, start_slot, group_size, 0)
    slot_ids = start_slot + jnp.arange(group_size, dtype=jnp.int32)
    live_mask = (slot_ids < live_count).astype(chosen.dtype)
    weights = chosen * live_mask[:, None, None]
    gathered = source[taken]
    pattern = "gji,gjw->giw" if flipped else "gij,gjw->giw"
    products = jnp.einsum(pattern, weights, gathered, preferred_element_type=jnp.float32)
    return jax.ops.segment_sum(products, placed, num_segments=seg_count)


def sparse_product(block_vals, take_ids, put_ids, live_count, source, seg_count, flipped):
    slot_total = block_vals.shape[0]
    group_size = min(8, slot_total)
    initial = jnp.zeros((seg_count, source.shape[1], source.shape[2]), jnp.float32)

    def advance(turn, accum):
        start_slot = (turn * group_size).astype(jnp.int32)
        return accum + block_term(
            block_vals,
            take_ids,
            put_ids,
            live_count,
            source,
            seg_count,
            flipped,
            start_slot,
            group_size,
        )

    return lax.fori_loop(0, slot_total // group_size, advance, initial)


def local(
    features, w_neigh, w_self, bias, cotangent, block_rows, block_cols, block_vals, block_count
):
    row_size = lax.axis_size("row")
    col_size = lax.axis_size("col")
    node_dev = features.shape[0]
    hidden_width = w_self.shape[1]
    values = block_vals[0, 0]
    row_ids = block_rows[0, 0]
    col_ids = block_cols[0, 0]
    live_count = block_count[0, 0]
    block_size = values.shape[1]
    slot_total = values.shape[0]
    rows_tile = node_dev * col_size
    cols_tile = node_dev * row_size
    row_index = lax.axis_index("row")
    col_index = lax.axis_index("col")
    owner_col = row_index * col_size // row_size
    is_self = (col_index == owner_col).astype(jnp.float32)
    offset = jnp.clip(row_index * rows_tile - col_index * cols_tile, 0, cols_tile - rows_tile)
    both_w = jnp.concatenate([w_neigh, w_self], axis=1)
    local_proj = jnp.dot(features, both_w, preferred_element_type=jnp.float32).astype(jnp.bfloat16)
    projected = lax.all_gather(local_proj, "row", axis=0, tiled=True)
    neigh_source = projected[:, :hidden_width].reshape(
        cols_tile // block_size, block_size, hidden_width
    )
    agg_part = sparse_product(
        values, col_ids, row_ids, live_count, neigh_source, rows_tile // block_size, False
    )
    agg_part = agg_part.reshape(rows_tile, hidden_width)
    own_rows = lax.dynamic_slice_in_dim(projected, offset, rows_tile, 0)[:, hidden_width:]
    live_mask = (jnp.arange(slot_total, dtype=jnp.int32) < live_count).astype(jnp.float32)
    row_mass = jnp.sum(values, axis=2, dtype=jnp.float32) * live_mask[:, None]
    row_sum = jax.ops.segment_sum(row_mass, row_ids, num_segments=rows_tile // block_size).reshape(
        rows_tile
    )
    self_part = own_rows.astype(jnp.float32) * is_self
    aggregate, own_term, degree = (
        lax.psum_scatter(agg_part, "col", scatter_dimension=0, tiled=True),
        lax.psum_scatter(self_part, "col", scatter_dimension=0, tiled=True),
        lax.psum_scatter(row_sum, "col", scatter_dimension=0, tiled=True),
    )
    inverse = 1.0 / (degree + 1.0)
    preact = own_term + aggregate * inverse[:, None] + bias
    output = jax.nn.elu(preact).astype(jnp.bfloat16)
    slopes = jnp.where(preact > 0, 1.0, jnp.exp(jnp.minimum(preact, 0.0)))
    grad_pre = cotangent.astype(jnp.float32) * slopes
    grad_round = grad_pre.astype(jnp.bfloat16)
    scaled = (grad_pre * inverse[:, None]).astype(jnp.bfloat16)
    group_scaled, group_grad = (
        lax.all_gather(scaled, "col", axis=0, tiled=True),
        lax.all_gather(grad_round, "col", axis=0, tiled=True),
    )
    back_source = group_scaled.reshape(rows_tile // block_size, block_size, hidden_width)
    back_part = sparse_product(
        values, row_ids, col_ids, live_count, back_source, cols_tile // block_size, True
    )
    back_part = back_part.reshape(cols_tile, hidden_width)
    self_back = jnp.zeros((cols_tile, hidden_width), jnp.float32)
    self_back = lax.dynamic_update_slice_in_dim(
        self_back, group_grad.astype(jnp.float32) * is_self, offset, 0
    )
    back_sum, self_sum = (
        lax.psum_scatter(back_part, "row", scatter_dimension=0, tiled=True),
        lax.psum_scatter(self_back, "row", scatter_dimension=0, tiled=True),
    )
    back = back_sum.astype(jnp.bfloat16)
    self_grad = self_sum.astype(jnp.bfloat16)
    part_self = jnp.einsum("nd,nh->dh", features, self_grad, preferred_element_type=jnp.float32)
    part_neigh = jnp.einsum("nd,nh->dh", features, back, preferred_element_type=jnp.float32)
    part_bias = jnp.sum(grad_pre, axis=0)
    total_self, total_neigh, total_bias = lax.psum(
        (part_self, part_neigh, part_bias), ("row", "col")
    )
    factor = 1.0 / math.sqrt(node_dev * row_size * col_size)
    grad_input = jnp.einsum("nh,dh->nd", self_grad, w_self, preferred_element_type=jnp.float32)
    grad_input = grad_input + jnp.einsum(
        "nh,dh->nd", back, w_neigh, preferred_element_type=jnp.float32
    )
    return (
        output,
        grad_input.astype(jnp.bfloat16),
        total_self * factor,
        total_neigh * (32.0 * factor),
        total_bias * factor,
    )


def solution(mesh):
    in_specs = (
        P(("col", "row"), None),
        P(),
        P(),
        P(),
        P(("row", "col"), None),
        P("row", "col", None),
        P("row", "col", None),
        P("row", "col", None, None, None),
        P("row", "col"),
    )
    out_specs = (P(("row", "col"), None), P(("col", "row"), None), P(), P(), P())
    return jax.shard_map(local, mesh=mesh, in_specs=in_specs, out_specs=out_specs, check_vma=False)
```

profile of v0, /device:TPU:1, one launch (start us, length us, event | category | flops | bytes accessed | tf_op | source)
XLA Modules:
  0.0 992.8 jit_solution(9653175240959098355)
XLA Ops:
  8.1 3.7 fusion.17
  11.9 64.5 %all-gather.4.cloned.1.call-done = bf16[2048,2048]{0,1:T(8,128)(2,1)} async-done(((bf16[128,2048]{0,1:T(8,128)(2,1)}), bf16[2048,2048]{0,1:T(8,128)(2,1)}) %all-gather.4.cloned.1.call-update) | async-done | bytes 8388624 | tf_op jit(solution)/shard_map/all_gather | solution.py:68
  76.4 4.7 convert_multiply_fusion.1
  81.2 4.7 slice.12
  85.9 6.4 copy.33
  94.8 199.8 %while.26 = (s32[]{:T(128)}, f32[8,128,1024]{2,1,0:T(8,128)}, s32[96]{0:T(128)S(1)}, bf16[96,128,128]{2,1,0:T(8,128)(2,1)}, s32[]{:T(128)}, /*index=5*/s32[96]{0...) while((s32[]{:T(128)}, f32[8,128,1024]{2,1,0:T(8,128)}, ...), condition=%wide.region_3.4_spmd, body=%wide.region_1.3_spmd.sunk | while | flops 269616192 | bytes 23335344 | solution.py:43
  98.4 3.7 fusion.52
  102.2 9.4 scatter_fusion
  115.3 3.7 fusion.52
  119.0 9.3 scatter_fusion
  132.0 3.7 fusion.52
  135.7 9.1 scatter_fusion
  148.7 3.7 fusion.52
  152.5 9.5 scatter_fusion
  165.6 3.7 fusion.52
  169.4 9.2 scatter_fusion
  182.3 3.7 fusion.52
  186.0 9.3 scatter_fusion
  198.9 3.7 fusion.52
  202.7 9.3 scatter_fusion
  215.6 3.7 fusion.52
  219.3 8.9 scatter_fusion
  231.9 3.7 fusion.52
  235.7 9.1 scatter_fusion
  248.3 3.7 fusion.52
  252.1 9.3 scatter_fusion
  265.0 3.7 fusion.52
  268.7 9.2 scatter_fusion
  281.6 3.7 fusion.52
  285.3 9.2 scatter_fusion
  294.5 5.4 copy.34
  309.2 19.1 %all-reduce = f32[1024]{0:T(1024)S(1)} all-reduce(f32[1024]{0:T(1024)S(1)} %bitcast.37), channel_id=4, replica_groups=mesh['row'=16,'col'=8] {'col'}, use_global_device_ids=true, to_apply=%region_7.8.clone | all-reduce | flops 1024 | bytes 8192
  328.3 54.7 %reduce-scatter.7.cloned.1.call-done = f32[128,1024]{0,1:T(8,128)} async-done(((f32[1024,1024]{0,1:T(8,128)}), f32[128,1024]{0,1:T(8,128)}) %reduce-scatter.7.cloned.1.call-update) | async-done | bytes 524304 | tf_op jit(solution)/shard_map/reduce_scatter | solution.py:84
  387.0 53.2 %all-gather.8.cloned.1.call-done = bf16[1024,1024]{0,1:T(8,128)(2,1)} async-done(((bf16[128,1024]{0,1:T(8,128)(2,1)}), bf16[1024,1024]{0,1:T(8,128)(2,1)}) %all-gather.8.cloned.1.call-update) | async-done | bytes 2097168 | tf_op jit(solution)/shard_map/all_gather | solution.py:96
  440.2 3.9 copy.35
  444.2 4.3 broadcast.79
  448.4 214.3 %while.27 = (s32[]{:T(128)}, f32[16,128,1024]{2,1,0:T(8,128)}, s32[96]{0:T(128)S(1)}, bf16[96,128,128]{1,2,0:T(8,128)(2,1)S(1)}, s32[]{:T(128)}, /*index=5*/s32[...) while((s32[]{:T(128)}, f32[16,128,1024]{2,1,0:T(8,128)}, ...), condition=%wide.region_11.12_spmd, body=%wide.region_9.11_spmd.sunk | while | flops 269616192 | bytes 48501220 | solution.py:43
  456.8 9.8 scatter_fusion.1
  471.3 3.6 fusion.55
  475.0 9.8 scatter_fusion.1
  489.4 3.6 fusion.55
  493.1 9.3 scatter_fusion.1
  507.1 3.6 fusion.55
  510.8 9.5 scatter_fusion.1
  524.9 3.6 fusion.55
  528.6 9.3 scatter_fusion.1
  546.2 9.3 scatter_fusion.1
  560.1 3.6 fusion.55
  563.9 9.4 scatter_fusion.1
  581.6 9.6 scatter_fusion.1
  599.6 9.7 scatter_fusion.1
  613.8 3.6 fusion.55
  617.6 9.5 scatter_fusion.1
  635.4 9.5 scatter_fusion.1
  649.4 3.6 fusion.55
  653.2 9.6 scatter_fusion.1
  663.0 4.1 convert_multiply_fusion
  667.2 4.3 broadcast_in_dim.51
  671.5 19.7 %dynamic_update_slice.3 = f32[2048,1024]{0,1:T(8,128)} dynamic-update-slice(f32[2048,1024]{0,1:T(8,128)} %broadcast_in_dim.51, f32[1024,1024]{0,1:T(8,128)} %convert_multiply_fusion, s32[]{:T(128)S(6)} %min.7, s32[]{:T(128)} %constant.109.clone.1) | dynamic-update-slice | bytes 8388612 | tf_op jit(solution)/shard_map/dynamic_update_slice | solution.py:105
  691.2 42.3 %reduce-scatter.11.cloned.1.call-done = f32[128,1024]{1,0:T(8,128)} async-done(((f32[2048,1024]{1,0:T(8,128)}), f32[128,1024]{1,0:T(8,128)}) %reduce-scatter.11.cloned.1.call-update) | async-done | bytes 524304 | tf_op jit(solution)/shard_map/reduce_scatter | solution.py:109
  736.8 72.4 %reduce-scatter.9.cloned.1.call-done = f32[128,1024]{0,1:T(8,128)} async-done(((f32[2048,1024]{0,1:T(8,128)}), f32[128,1024]{0,1:T(8,128)}) %reduce-scatter.9.cloned.1.call-update) | async-done | bytes 524304 | tf_op jit(solution)/shard_map/reduce_scatter | solution.py:110
  814.2 68.2 %psum.23 = f32[1024]{0:T(1024)S(1)} all-reduce(f32[1024]{0:T(1024)S(1)} %get-tuple-element.323), channel_id=1, replica_groups=mesh['row'=16,'col'=8] {'row','col'}, use_global_device_ids=true, to_apply=%region_16.17 | all-reduce | flops 1024 | bytes 8192 | tf_op jit(solution)/shard_map/psum | solution.py:117
  885.2 90.0 %all-reduce.4.cloned.1.call-done = (f32[768,1024]{0,1:T(8,128)}, f32[768,1024]{0,1:T(8,128)}) async-done(((f32[768,1024]{0,1:T(8,128)}, f32[768,1024]{0,1:T(8,128)}), (f32[768,1024]{0,1:T(8,128)}, f32[768,1024]{0,1:T(8,128)})) %all-reduce.4.cloned.1.call-update) | async-done | bytes 6291472 | tf_op jit(solution)/shard_map/psum | solution.py:117
  975.1 4.9 broadcast_multiply_fusion
  (229 shorter events, 151.6 us)
Async XLA Ops:
  7.2 0.9 copy-start
  7.2 69.2 %all-gather.4.cloned.1.call-start = ((), (), s32[]{:S(2)}) async-start(), calls=%async_computation.4 | async-start | bytes 8912896 | tf_op jit(solution)/shard_map/all_gather | solution.py:68
  11.8 316.5 %reduce-scatter.5.cloned.1.call-start = ((), (), s32[]{:S(2)}) async-start(), calls=%async_computation.5 | async-start | bytes 4718592 | tf_op jit(solution)/shard_map/reduce_scatter | solution.py:85
  81.1 301.9 %reduce-scatter.7.cloned.1.call-start = ((), (), s32[]{:S(2)}) async-start(), calls=%async_computation.6 | async-start | bytes 4718592 | tf_op jit(solution)/shard_map/reduce_scatter | solution.py:84
  92.3 2.5 copy-start.9
  92.3 2.5 copy-start.10
  299.9 4.2 copy-start.11
  299.9 140.3 %all-gather.8.cloned.1.call-start = ((), (), s32[]{:S(2)}) async-start(), calls=%async_computation.9 | async-start | bytes 2359296 | tf_op jit(solution)/shard_map/all_gather | solution.py:96
  303.5 79.6 %copy-start.8 = (f32[1024]{0:T(1024)S(1)}, f32[1024]{0:T(1024)}, u32[]{:S(2)}) copy-start(f32[1024]{0:T(1024)} %param.16) | copy-start | bytes 12292
  386.4 276.7 %all-gather.6.cloned.1.call-start = ((), (), s32[]{:S(2)}) async-start(), calls=%async_computation.7 | async-start | bytes 2359296 | tf_op jit(solution)/shard_map/all_gather | solution.py:97
  386.9 346.6 %reduce-scatter.11.cloned.1.call-start = ((), (), s32[]{:S(2)}) async-start(), calls=%async_computation.10 | async-start | bytes 8912896 | tf_op jit(solution)/shard_map/reduce_scatter | solution.py:109
  448.4 1.7 copy-start.1
  456.8 9.8 copy-start.2
  466.7 1.7 copy-start.1
  475.0 9.8 copy-start.2
  484.8 1.7 copy-start.1
  493.1 9.3 copy-start.2
  502.5 1.7 copy-start.1
  510.8 9.5 copy-start.2
  520.3 1.7 copy-start.1
  528.6 9.3 copy-start.2
  537.9 1.7 copy-start.1
  546.2 9.3 copy-start.2
  555.5 1.7 copy-start.1
  563.9 9.4 copy-start.2
  573.3 1.7 copy-start.1
  581.6 9.6 copy-start.2
  591.2 1.7 copy-start.1
  599.5 9.7 copy-start.2
  609.2 1.7 copy-start.1
  617.6 9.5 copy-start.2
  627.0 1.7 copy-start.1
  635.4 9.5 copy-start.2
  644.8 1.7 copy-start.1
  653.2 9.6 copy-start.2
  662.8 146.4 %reduce-scatter.9.cloned.1.call-start = ((), (), s32[]{:S(2)}) async-start(), calls=%async_computation.8 | async-start | bytes 8912896 | tf_op jit(solution)/shard_map/reduce_scatter | solution.py:110
  691.1 284.0 %all-reduce.4.cloned.1.call-start = ((), (), s32[]{:S(2)}) async-start(), calls=%async_computation.11 | async-start | bytes 12582912 | tf_op jit(solution)/shard_map/psum | solution.py:117
  812.4 0.9 copy-start.7
  812.4 70.6 %copy-start.3 = (f32[128,1024]{0,1:T(8,128)S(1)}, f32[128,1024]{0,1:T(8,128)}, u32[]{:S(2)}) copy-start(f32[128,1024]{0,1:T(8,128)} %reduce-scatter.9.cloned.1.call-done) | copy-start | bytes 1572868
  812.4 70.6 %copy-start.5 = (bf16[768,1024]{1,0:T(8,128)(2,1)S(1)}, bf16[768,1024]{1,0:T(8,128)(2,1)}, u32[]{:S(2)}) copy-start(bf16[768,1024]{1,0:T(8,128)(2,1)} %param.15) | copy-start | bytes 4718596
  812.4 71.2 %copy-start.4 = (f32[128,1024]{1,0:T(8,128)S(1)}, f32[128,1024]{1,0:T(8,128)}, u32[]{:S(2)}) copy-start(f32[128,1024]{1,0:T(8,128)} %reduce-scatter.11.cloned.1.call-done) | copy-start | bytes 1572868
  882.4 1.4 copy-start.6
Sparse Core Ops, SparseCore 0:
  11.9 64.4 all-gather.3
  81.2 82.5 reduce-scatter.4
  300.0 82.9 reduce-scatter.6
  386.5 53.6 all-gather.7
  442.3 52.2 all-gather.5
  662.9 70.5 reduce-scatter.10
  735.9 73.2 reduce-scatter.8
  814.7 160.4 all-reduce.3
where the time goes:
time: 996 us; the launch traced here: 993 us
  waiting for transfers between devices  378 us (38%)
  other arithmetic  262 us (26%)
  local copies, waits for them, and re-layouts  149 us (15%)
  matrix products  100 us (10%)
  blocking collectives  87.2 us (9%)
  between operations  15.6 us (2%)
    scatter-add x24, other arithmetic, block_term(): return jax.ops.segment_sum(products, placed, num_segments=seg_count)  225 us
    psum x1, waiting for transfers between devices, local(): lax.psum((part_self, part_neigh, part_bias), ('row', 'col'))  90 us
    dot_general x24, matrix products, block_term(): jnp.einsum(pattern, weights, gathered, preferred_element_type=jnp.float32)  88 us
    reduce_scatter x1, waiting for transfers between devices, local(): lax.psum_scatter(self_back, 'row', scatter_dimension=0, tiled=True)  72.4 us
    psum x1, blocking collectives, local(): lax.psum((part_self, part_neigh, part_bias), ('row', 'col'))  68.2 us
    all_gather x1, waiting for transfers between devices, local(): projected = lax.all_gather(local_proj, 'row', axis=0, tiled=True)  64.5 us
    gather x24, local copies, waits for them, and re-layouts, block_term(): gathered = source[taken]  62.2 us
    reduce_scatter x1, waiting for transfers between devices, local(): lax.psum_scatter(agg_part, 'col', scatter_dimension=0, tiled=True)  54.7 us
  transfers between devices with their start and end apart: 8, of which 6 were waited for; matrix products, arithmetic and copies ran while one was open for 47% of the time, Pallas kernels for 0%

commit v1 on v0

v1 whole, which is shorter than its diff:
```python
import math

import jax
import jax.numpy as jnp
from jax import lax
from jax.experimental import pallas as pl
from jax.experimental.pallas import tpu as pltpu
from jax.sharding import PartitionSpec as P


def densify_kernel(rows_ref, cols_ref, count_ref, vals_ref, tile_ref, mass_ref, acc):
    row_blocks, col_blocks, size, _ = acc.shape

    def clear(i, carry):
        for j in range(col_blocks):
            acc[i, j] = jnp.zeros((size, size), jnp.float32)
        return carry

    lax.fori_loop(0, row_blocks, clear, 0)

    def add(s, carry):
        i = rows_ref[s]
        j = cols_ref[s]
        acc[i, j] += vals_ref[s].astype(jnp.float32)
        return carry

    lax.fori_loop(0, count_ref[0], add, 0)
    diagonal = lax.broadcasted_iota(jnp.int32, (size, size), 0) == lax.broadcasted_iota(
        jnp.int32, (size, size), 1
    )

    def finish(i, carry):
        total = jnp.zeros((size, size), jnp.float32)
        start = pl.multiple_of(i * size, size)
        for j in range(col_blocks):
            block = acc[i, j]
            total = total + block
            tile_ref[pl.ds(start, size), j * size : (j + 1) * size] = block.astype(jnp.bfloat16)
        sums = jnp.sum(total, axis=1, keepdims=True)
        as_row = jnp.sum(jnp.where(diagonal, sums, 0.0), axis=0, keepdims=True)
        mass_ref[i] = jnp.broadcast_to(as_row, (8, size))
        return carry

    lax.fori_loop(0, row_blocks, finish, 0)


def densify(values, row_ids, col_ids, live_count, row_blocks, col_blocks):
    size = values.shape[1]
    smem = pl.BlockSpec(memory_space=pltpu.SMEM)
    vmem = pl.BlockSpec(memory_space=pltpu.VMEM)
    return pl.pallas_call(
        densify_kernel,
        out_shape=(
            jax.ShapeDtypeStruct((row_blocks * size, col_blocks * size), jnp.bfloat16),
            jax.ShapeDtypeStruct((row_blocks, 8, size), jnp.float32),
        ),
        in_specs=[smem, smem, smem, vmem],
        out_specs=(vmem, vmem),
        scratch_shapes=[pltpu.VMEM((row_blocks, col_blocks, size, size), jnp.float32)],
        compiler_params=pltpu.CompilerParams(vmem_limit_bytes=40 * 1024 * 1024),
        name="densify",
    )(row_ids, col_ids, live_count, values)


def matmul(a, b, contract):
    return lax.dot_general(a, b, ((contract[0], contract[1]), ((), ())), preferred_element_type=jnp.float32)


def local(
    features, w_neigh, w_self, bias, cotangent, block_rows, block_cols, block_vals, block_count
):
    row_size = lax.axis_size("row")
    col_size = lax.axis_size("col")
    node_dev = features.shape[0]
    values = block_vals[0, 0]
    tile, mass = densify(
        values, block_rows[0, 0], block_cols[0, 0], block_count[0], col_size, row_size
    )
    to_out = [
        (r * col_size + c, c * row_size + r) for r in range(row_size) for c in range(col_size)
    ]
    to_in = [(d, s) for s, d in to_out]
    own_feat = lax.ppermute(features, ("row", "col"), to_out)
    gathered = lax.all_gather(features, "row", axis=0, tiled=True)
    part = matmul(tile, gathered, ((1,), (0,)))
    mixed = lax.psum_scatter(part, "col", scatter_dimension=0, tiled=True)
    degree = lax.psum_scatter(mass[:, 0, :], "col", scatter_dimension=0, tiled=True)[0]
    high = mixed.astype(jnp.bfloat16)
    low = (mixed - high.astype(jnp.float32)).astype(jnp.bfloat16)
    aggregate = matmul(high, w_neigh, ((1,), (0,))) + matmul(low, w_neigh, ((1,), (0,)))
    own = matmul(own_feat, w_self, ((1,), (0,))).astype(jnp.bfloat16).astype(jnp.float32)
    inverse = 1.0 / (degree + 1.0)
    preact = own + aggregate * inverse[:, None] + bias
    output = jax.nn.elu(preact).astype(jnp.bfloat16)
    slopes = jnp.where(preact > 0, 1.0, jnp.exp(jnp.minimum(preact, 0.0)))
    grad_pre = cotangent.astype(jnp.float32) * slopes
    grad_round = grad_pre.astype(jnp.bfloat16)
    scaled = (grad_pre * inverse[:, None]).astype(jnp.bfloat16)
    part_self = matmul(own_feat, grad_round, ((0,), (0,)))
    part_neigh = matmul(high, scaled, ((0,), (0,)))
    part_bias = jnp.sum(grad_pre, axis=0)
    total_self, total_neigh, total_bias = lax.psum(
        (part_self, part_neigh, part_bias), ("row", "col")
    )
    back_in = matmul(scaled, w_neigh, ((1,), (1,))).astype(jnp.bfloat16)
    self_in = matmul(grad_round, w_self, ((1,), (1,)))
    self_in = lax.ppermute(self_in, ("row", "col"), to_in)
    back_all = lax.all_gather(back_in, "col", axis=0, tiled=True)
    back_part = matmul(tile, back_all, ((0,), (0,)))
    back = lax.psum_scatter(back_part, "row", scatter_dimension=0, tiled=True)
    grad_input = (back + self_in).astype(jnp.bfloat16)
    factor = 1.0 / math.sqrt(node_dev * row_size * col_size)
    return (
        output,
        grad_input,
        total_self * factor,
        total_neigh * (32.0 * factor),
        total_bias * factor,
    )


def solution(mesh):
    in_specs = (
        P(("col", "row"), None),
        P(),
        P(),
        P(),
        P(("row", "col"), None),
        P("row", "col", None),
        P("row", "col", None),
        P("row", "col", None, None, None),
        P("row", "col"),
    )
    out_specs = (P(("row", "col"), None), P(("col", "row"), None), P(), P(), P())
    return jax.shard_map(local, mesh=mesh, in_specs=in_specs, out_specs=out_specs, check_vma=False)
```

time: 996 us -> 458 us (0.46)
  other arithmetic: 262 us -> 10.8 us
  local copies, waits for them, and re-layouts: 149 us -> 10.2 us
  waiting for transfers between devices: 378 us -> 278 us
  matrix products: 100 us -> 30 us
  blocking collectives: 87.2 us -> 99.5 us
    scatter-add x25 -> x0, other arithmetic: 226 us -> none  [the longest x24 225 us: block_term(): return jax.ops.segment_sum(products, placed, num_segments=seg_count)]
    dot_general x29 -> x9, matrix products: 100 us -> 30 us  [matmul(): lax.dot_general(a, b, ((contract[0], contract[1]), ((), ())), preferred_e...]
    gather x24 -> x0, local copies, waits for them, and re-layouts: 62.2 us -> none  [block_term(): gathered = source[taken]]
    reduce_scatter x4 -> x2, waiting for transfers between devices: 169 us -> 115 us  [the longest x1 59.1 us: local(): mixed = lax.psum_scatter(part, 'col', scatter_dimension=0, tiled=True)]
    all_gather x3 -> x2, waiting for transfers between devices: 118 us -> 75.7 us  [the longest x1 43.3 us: local(): back_all = lax.all_gather(back_in, 'col', axis=0, tiled=True)]
    while x50 -> x0, local copies, waits for them, and re-layouts: 29.3 us -> none
    dynamic_update_slice x1 -> x0, local copies, waits for them, and re-layouts: 19.7 us -> none  [local(): lax.dynamic_update_slice_in_dim(self_back, group_grad.astype(jnp.float32)...]
    convert_element_type x26 -> x1, other arithmetic: 16.5 us -> 1.71 us  [local(): grad_input = (back + self_in).astype(jnp.bfloat16)]
  transfers between devices with their start and end apart: 8 -> 7, of which waited for: 6 -> 5; matrix products, arithmetic and copies ran while one was open for 47% -> 7% of each run, Pallas kernels for 0% -> 1%
where the time goes in v1:
time: 458 us; the launch traced here: 454 us
  waiting for transfers between devices  278 us (61%)
  blocking collectives  99.5 us (22%)
  matrix products  30 us (7%)
  between operations  14.6 us (3%)
  other arithmetic  10.8 us (2%)
  local copies, waits for them, and re-layouts  10.2 us (2%)
  starting transfers between devices  7.98 us (2%)
    psum x1, waiting for transfers between devices, local(): lax.psum((part_self, part_neigh, part_bias), ('row', 'col'))  86.1 us
    psum x1, blocking collectives, local(): lax.psum((part_self, part_neigh, part_bias), ('row', 'col'))  79.3 us
    reduce_scatter x1, waiting for transfers between devices, local(): mixed = lax.psum_scatter(part, 'col', scatter_dimension=0, tiled=True)  59.1 us
    reduce_scatter x1, waiting for transfers between devices, local(): back = lax.psum_scatter(back_part, 'row', scatter_dimension=0, tiled=True)  56.1 us
    all_gather x1, waiting for transfers between devices, local(): back_all = lax.all_gather(back_in, 'col', axis=0, tiled=True)  43.3 us
    all_gather x1, waiting for transfers between devices, local(): gathered = lax.all_gather(features, 'row', axis=0, tiled=True)  32.5 us
    dot_general x9, matrix products, matmul(): lax.dot_general(a, b, ((contract[0], contract[1]), ((), ())), preferred_e...  30 us
    unnamed x1, blocking collectives  20.2 us
  transfers between devices with their start and end apart: 7, of which 5 were waited for; matrix products, arithmetic and copies ran while one was open for 7% of the time, Pallas kernels for 1%

profile of v1, /device:TPU:1, one launch (start us, length us, event | category | flops | bytes accessed | tf_op | source)
XLA Modules:
  0.0 454.0 jit_solution(5979370912681541841)
XLA Ops:
  7.2 0.0 copy-start
  7.2 0.0 all-gather.3.cloned.1.call-start
  7.2 0.7 all-gather.3.cloned.1.call-update
  7.9 0.0 reduce-scatter.3.cloned.1.call-start
  8.6 0.0 copy-start.1
  8.6 1.9 copy-done.1
  10.5 0.0 copy-start.2
  10.5 0.7 copy-done.2
  11.2 0.0 copy-start.3
  11.2 0.7 copy-done.3
  11.8 3.1 densify.1
  14.9 0.0 copy-start.4
  14.9 2.0 copy-done.4
  17.0 32.5 %all-gather.3.cloned.1.call-done = bf16[2048,768]{1,0:T(8,128)(2,1)} async-done(((bf16[128,768]{1,0:T(8,128)(2,1)}), bf16[2048,768]{1,0:T(8,128)(2,1)}) %all-gather.3.cloned.1.call-update) | async-done | bytes 3145744 | tf_op jit(solution)/shard_map/all_gather | solution.py:84
  49.4 8.2 %fusion.22 = f32[1024,768]{1,0:T(8,128)} fusion(bf16[1024,2048]{1,0:T(8,128)(2,1)} %copy-done.4, bf16[2048,768]{1,0:T(8,128)(2,1)} %all-gather.3.cloned.1.call-done), kind=kOutput, calls=%fused_computation.32 | convolution fusion | flops 3221225472 | bytes 10485760 | tf_op jit(solution)/shard_map/dot_general | solution.py:66
  57.7 0.0 copy-start.11
  57.7 0.0 copy-start.5
  57.7 0.0 reduce-scatter.3.cloned.1.call-update
  57.7 0.0 copy-start.8
  57.7 0.0 copy-start.10
  57.7 0.0 all-gather.5.cloned.1.call-start
  57.8 4.6 %collective-permute-start = (bf16[128,768]{1,0:T(8,128)(2,1)}, bf16[128,768]{1,0:T(8,128)(2,1)}, u32[]{:S(2)}, u32[]{:S(2)}) collective-permute-start(bf16[128,768]{1,0:T(8,128)(2,1)} %param.9), channel_id=1, source_target_pairs={{0,0},{1,16},{2,32},{3,48},{4,64},{5,80},{6,96},{7,112},{8,1},{9,1... | collective-permute-start | bytes 589832 | tf_op jit(solution)/shard_map/ppermute | solution.py:83
  62.4 0.0 copy-done.11
  62.4 0.6 dynamic-slice
  63.0 20.2 %all-reduce = f32[8,128]{1,0:T(8,128)S(1)} all-reduce(f32[8,128]{1,0:T(8,128)S(1)} %bitcast.25), channel_id=3, replica_groups=mesh['row'=16,'col'=8] {'col'}, use_global_device_ids=true, to_apply=%region_1.0.clone | all-reduce | flops 1024 | bytes 8192
  83.2 0.7 fusion.11
  83.8 59.1 %reduce-scatter.3.cloned.1.call-done = f32[128,768]{1,0:T(8,128)} async-done(((f32[1024,768]{1,0:T(8,128)}), f32[128,768]{1,0:T(8,128)}) %reduce-scatter.3.cloned.1.call-update) | async-done | bytes 393232 | tf_op jit(solution)/shard_map/reduce_scatter | solution.py:86
  143.0 0.0 copy-done.5
  143.0 1.4 fusion.15
  144.4 1.5 fusion
  145.9 0.0 collective-permute-done
  145.9 0.0 copy-done
  145.9 0.0 copy-done.8
  145.9 0.0 copy-done.10
  145.9 2.2 fusion.19
  148.1 0.0 copy-start.6
  148.1 0.8 copy-done.6
  148.9 1.4 convolution_convert_fusion.1
  150.3 0.0 copy-start.7
  150.3 0.0 copy-start.9
  150.3 0.0 all-gather.5.cloned.1.call-update
  150.3 0.0 all-reduce.4.cloned.1.call-start
  150.4 3.4 convolution_bitcast_fusion
  153.8 0.0 copy-done.7
  153.8 0.0 copy-done.9
  153.8 2.4 fusion.12
  156.2 0.0 all-reduce.4.cloned.1.call-update
  156.2 0.0 reduce-scatter.5.cloned.1.call-start
  156.3 43.3 %all-gather.5.cloned.1.call-done = bf16[1024,768]{1,0:T(8,128)(2,1)} async-done(((bf16[128,768]{1,0:T(8,128)(2,1)}), bf16[1024,768]{1,0:T(8,128)(2,1)}) %all-gather.5.cloned.1.call-update) | async-done | bytes 1572880 | tf_op jit(solution)/shard_map/all_gather | solution.py:108
  199.5 8.8 %fusion.23 = f32[2048,768]{1,0:T(8,128)} fusion(bf16[1024,2048]{1,0:T(8,128)(2,1)} %copy-done.4, bf16[1024,768]{1,0:T(8,128)(2,1)} %all-gather.5.cloned.1.call-done), kind=kOutput, calls=%fused_computation.33 | convolution fusion | flops 3221225472 | bytes 12058624 | tf_op jit(solution)/shard_map/dot_general | solution.py:66
  208.4 0.0 reduce-scatter.5.cloned.1.call-update
  208.4 0.7 fusion.8
  209.1 3.2 collective-permute-start.1
  212.2 79.3 %psum.23 = f32[1024]{0:T(1024)S(1)} all-reduce(f32[1024]{0:T(1024)S(1)} %get-tuple-element.21), channel_id=1, replica_groups=mesh['row'=16,'col'=8] {'row','col'}, use_global_device_ids=true, to_apply=%region_6.7 | all-reduce | flops 1024 | bytes 8192 | tf_op jit(solution)/shard_map/psum | solution.py:102
  291.5 0.6 broadcast_multiply_fusion.2
  292.1 86.1 %all-reduce.4.cloned.1.call-done = (f32[768,1024]{0,1:T(8,128)}, f32[768,1024]{1,0:T(8,128)}) async-done(((f32[768,1024]{0,1:T(8,128)}, f32[768,1024]{1,0:T(8,128)}), (f32[768,1024]{0,1:T(8,128)}, f32[768,1024]{1,0:T(8,128)})) %all-reduce.4.cloned.1.call-update) | async-done | bytes 6291472 | tf_op jit(solution)/shard_map/psum | solution.py:102
  378.2 3.8 broadcast_multiply_fusion.1
  382.0 3.5 copy.15
  385.5 4.1 broadcast_multiply_fusion
  389.7 0.0 collective-permute-done.1
  389.7 56.1 %reduce-scatter.5.cloned.1.call-done = f32[128,768]{1,0:T(8,128)} async-done(((f32[2048,768]{1,0:T(8,128)}), f32[128,768]{1,0:T(8,128)}) %reduce-scatter.5.cloned.1.call-update) | async-done | bytes 393232 | tf_op jit(solution)/shard_map/reduce_scatter | solution.py:110
  445.8 1.7 add_convert_fusion
  (1 shorter events, 0.0 us)
Async XLA Ops:
  7.2 138.7 %copy-start = (bf16[768,1024]{1,0:T(8,128)(2,1)S(1)}, bf16[768,1024]{1,0:T(8,128)(2,1)}, u32[]{:S(2)}) copy-start(bf16[768,1024]{1,0:T(8,128)(2,1)} %param.11) | copy-start | bytes 4718596
  7.2 42.2 %all-gather.3.cloned.1.call-start = ((), (), s32[]{:S(2)}) async-start(), calls=%async_computation.2 | async-start | bytes 3342336 | tf_op jit(solution)/shard_map/all_gather | solution.py:84
  7.9 135.1 %reduce-scatter.3.cloned.1.call-start = ((), (), s32[]{:S(2)}) async-start(), calls=%async_computation.3 | async-start | bytes 3538944 | tf_op jit(solution)/shard_map/reduce_scatter | solution.py:86
  8.6 1.9 copy-start.1
  10.5 0.7 copy-start.2
  11.2 0.7 copy-start.3
  14.9 2.0 copy-start.4
  57.7 4.8 %copy-start.11 = (u32[128]{0:T(128)S(1)}, u32[128]{0:T(128)}, u32[]{:S(2)}) copy-start(u32[128]{0:T(128)} %constant.21) | copy-start | bytes 1540
  57.7 85.3 %copy-start.5 = (bf16[768,1024]{1,0:T(8,128)(2,1)S(1)}, bf16[768,1024]{1,0:T(8,128)(2,1)}, u32[]{:S(2)}) copy-start(bf16[768,1024]{1,0:T(8,128)(2,1)} %param.10) | copy-start | bytes 4718596
  57.7 88.2 %copy-start.8 = (bf16[128,1024]{1,0:T(8,128)(2,1)S(1)}, bf16[128,1024]{1,0:T(8,128)(2,1)}, u32[]{:S(2)}) copy-start(bf16[128,1024]{1,0:T(8,128)(2,1)} %param.13) | copy-start | bytes 786436
  57.7 88.2 %copy-start.10 = (f32[1024]{0:T(1024)S(1)}, f32[1024]{0:T(1024)}, u32[]{:S(2)}) copy-start(f32[1024]{0:T(1024)} %param.12) | copy-start | bytes 12292
  57.7 141.8 %all-gather.5.cloned.1.call-start = ((), (), s32[]{:S(2)}) async-start(), calls=%async_computation.4 | async-start | bytes 1769472 | tf_op jit(solution)/shard_map/all_gather | solution.py:108
  57.8 88.1 %collective-permute-start = (bf16[128,768]{1,0:T(8,128)(2,1)}, bf16[128,768]{1,0:T(8,128)(2,1)}, u32[]{:S(2)}, u32[]{:S(2)}) collective-permute-start(bf16[128,768]{1,0:T(8,128)(2,1)} %param.9), channel_id=1, source_target_pairs={{0,0},{1,16},{2,32},{3,48},{4,64},{5,80},{6,96},{7,112},{8,1},{9,1... | collective-permute-start | bytes 589832 | tf_op jit(solution)/shard_map/ppermute | solution.py:83
  148.1 0.8 copy-start.6
  150.3 3.5 copy-start.7
  150.3 3.5 copy-start.9
  150.3 227.9 %all-reduce.4.cloned.1.call-start = ((), (), s32[]{:S(2)}) async-start(), calls=%async_computation.6 | async-start | bytes 12582912 | tf_op jit(solution)/shard_map/psum | solution.py:102
  156.2 289.6 %reduce-scatter.5.cloned.1.call-start = ((), (), s32[]{:S(2)}) async-start(), calls=%async_computation.5 | async-start | bytes 6684672 | tf_op jit(solution)/shard_map/reduce_scatter | solution.py:110
  209.1 180.6 %collective-permute-start.1 = (f32[128,768]{1,0:T(8,128)S(1)}, f32[128,768]{1,0:T(8,128)S(1)}, u32[]{:S(2)}, u32[]{:S(2)}) collective-permute-start(f32[128,768]{1,0:T(8,128)S(1)} %fusion.8), channel_id=1, source_target_pairs={{0,0},{16,1},{32,2},{48,3},{64,4},{80,5},{96,6},{112,7},{1,8},{17,... | collective-permute-start | bytes 1179656 | tf_op jit(solution)/shard_map/ppermute | solution.py:107
Sparse Core Ops, SparseCore 0:
  9.7 39.6 all-gather.2
  57.8 85.1 reduce-scatter.2
  150.5 49.0 all-gather.4
  204.9 173.3 all-reduce.3
  380.5 65.2 reduce-scatter.4

commit v2 on v1

v2 whole, which is shorter than its diff:
```python
import math

import jax
import jax.numpy as jnp
from jax import lax
from jax.experimental import pallas as pl
from jax.experimental.pallas import tpu as pltpu
from jax.sharding import PartitionSpec as P


def densify_kernel(rows_ref, cols_ref, count_ref, vals_ref, tile_ref, mass_ref, acc):
    row_blocks, col_blocks, size, _ = acc.shape

    def clear(i, carry):
        for j in range(col_blocks):
            acc[i, j] = jnp.zeros((size, size), jnp.float32)
        return carry

    lax.fori_loop(0, row_blocks, clear, 0)

    def add(s, carry):
        i = rows_ref[s]
        j = cols_ref[s]
        acc[i, j] += vals_ref[s].astype(jnp.float32)
        return carry

    lax.fori_loop(0, count_ref[0], add, 0)
    diagonal = lax.broadcasted_iota(jnp.int32, (size, size), 0) == lax.broadcasted_iota(
        jnp.int32, (size, size), 1
    )

    def finish(i, carry):
        total = jnp.zeros((size, size), jnp.float32)
        start = pl.multiple_of(i * size, size)
        for j in range(col_blocks):
            block = acc[i, j]
            total = total + block
            tile_ref[pl.ds(start, size), j * size : (j + 1) * size] = block.astype(jnp.bfloat16)
        sums = jnp.sum(total, axis=1, keepdims=True)
        as_row = jnp.sum(jnp.where(diagonal, sums, 0.0), axis=0, keepdims=True)
        mass_ref[i] = jnp.broadcast_to(as_row, (8, size))
        return carry

    lax.fori_loop(0, row_blocks, finish, 0)


def densify(values, row_ids, col_ids, live_count, row_blocks, col_blocks):
    size = values.shape[1]
    smem = pl.BlockSpec(memory_space=pltpu.SMEM)
    vmem = pl.BlockSpec(memory_space=pltpu.VMEM)
    return pl.pallas_call(
        densify_kernel,
        out_shape=(
            jax.ShapeDtypeStruct((row_blocks * size, col_blocks * size), jnp.bfloat16),
            jax.ShapeDtypeStruct((row_blocks, 8, size), jnp.float32),
        ),
        in_specs=[smem, smem, smem, vmem],
        out_specs=(vmem, vmem),
        scratch_shapes=[pltpu.VMEM((row_blocks, col_blocks, size, size), jnp.float32)],
        compiler_params=pltpu.CompilerParams(vmem_limit_bytes=40 * 1024 * 1024),
        name="densify",
    )(row_ids, col_ids, live_count, values)


MESH = pl.DeviceIdType.MESH
BF = jnp.bfloat16
F32 = jnp.float32


def remote(src, dst, send, recv, device):
    return pltpu.make_async_remote_copy(
        src_ref=src, dst_ref=dst, send_sem=send, recv_sem=recv, device_id=device, device_id_type=MESH
    )


def layer_kernel(
    tile_hbm, mass, features, wn_hbm, ws_hbm, bias, cotangent,
    out_ref, gin_ref, gself_ref, gneigh_ref, gbias_ref,
    tile, wn, ws, local_sem,
    fg, acc, own_feat, send_blocks, recv_blocks, recv_mass, mixed,
    scaled, grounded, sgt, tblock, trecv,
    x_mine, y_mine, x_other, y_other, other, other_recv, partial,
    r1, q1, r2, q2, r3, result, result2,
    halves, pair_recv, row_send, row_recv,
    bsum, bx, by, bz, bk,
    ag_s, ag_r, fw_s, fw_r, pm_s, pm_r, rs_s, rs_r, ms_s, ms_r, sg_s, sg_r, t_s, t_r,
    ot_s, ot_r, a1_s, a1_r, a2_s, a2_r, a3_s, a3_r, g3_s, g3_r, g2_s, g2_r, g1_s, g1_r, fin_s, fin_r,
    b_s, b_r, pd_s, pd_r, br_s, br_r,
):
    r = lax.axis_index("row")
    c = lax.axis_index("col")
    xl, z, core = r // 8, (r // 2) % 4, r % 2
    y, xh = c // 2, c % 2
    x = xh * 2 + xl

    def at_row(chip, k):
        return (chip * 2 + k, c)

    def chip_fwd(k):
        return ((xl + k // 4) % 2) * 4 + (z + k) % 4

    def chip_back(k):
        return ((xl + 2 - k // 4) % 2) * 4 + (z + 8 - k) % 4

    def device_of(px, py, pz):
        return (((px % 2) * 4 + pz) * 2 + core, py * 2 + px // 2)

    here = (x, y, z)
    axis_orders = ((0, 1, 2), (1, 2, 0), (2, 0, 1))

    def along(axis, d):
        spot = list(here)
        spot[axis] = (spot[axis] + d) % 4
        return device_of(*spot)

    partner = (r + 1 - 2 * core, c)
    node = c * 16 + r
    out_dev = (node // 8, node % 8)
    block = r * 8 + c
    in_dev = (block % 16, block // 16)
    moved = node != block

    copies = [
        pltpu.make_async_copy(tile_hbm, tile, local_sem.at[0]),
        pltpu.make_async_copy(ws_hbm, ws, local_sem.at[1]),
        pltpu.make_async_copy(wn_hbm, wn, local_sem.at[2]),
    ]
    for copy in copies:
        copy.start()

    barrier = pltpu.get_barrier_semaphore()

    def hello(device):
        pl.semaphore_signal(barrier, inc=1, device_id=device, device_id_type=MESH)

    def hello_row(k, carry):
        hello(at_row(chip_fwd(k), core))
        return carry

    def hello_col(k, carry):
        hello((r, (c + k) % 8))
        return carry

    lax.fori_loop(1, 8, hello_row, 0)
    lax.fori_loop(1, 8, hello_col, 0)
    hello(partner)
    hello((((1 - xl) * 4 + z) * 2 + core, y * 2 + 1 - xh))

    @pl.when(moved)
    def _():
        hello(out_dev)
        hello(in_dev)
        pl.semaphore_wait(barrier, 18)

    @pl.when(jnp.logical_not(moved))
    def _():
        pl.semaphore_wait(barrier, 16)

    def gather_send(k):
        return remote(
            features, fg.at[pl.ds(r * 128, 128)], ag_s.at[k], ag_r.at[k], at_row(chip_fwd(k), core)
        )

    def gather_recv(k):
        rows = pl.ds((chip_back(k) * 2 + core) * 128, 128)
        return remote(features, fg.at[rows], ag_s.at[k], ag_r.at[k], at_row(chip_back(k), core))

    def forward(k):
        rows = pl.ds((chip_back(k) * 2 + core) * 128, 128)
        return remote(fg.at[rows], fg.at[rows], fw_s.at[k], fw_r.at[k], partner)

    def forward_recv(k):
        rows = pl.ds((chip_back(k) * 2 + 1 - core) * 128, 128)
        return remote(fg.at[rows], fg.at[rows], fw_s.at[k], fw_r.at[k], partner)

    def permute():
        return remote(features, own_feat, pm_s.at[0], pm_r.at[0], out_dev)

    def mass_send(k):
        to = (c + k) % 8
        return remote(mass.at[to], recv_mass.at[k - 1], ms_s.at[k], ms_r.at[k], (r, to))

    def start_gather(k, carry):
        gather_send(k).start()
        return carry

    lax.fori_loop(1, 8, start_gather, 0)

    @pl.when(moved)
    def _():
        permute().start()

    @pl.when(jnp.logical_not(moved))
    def _():
        own_feat[...] = features[...]

    def start_mass(k, carry):
        mass_send(k).start()
        return carry

    lax.fori_loop(1, 8, start_mass, 0)
    fg[pl.ds(r * 128, 128), :] = features[...]

    def clear(i, carry):
        acc[pl.ds(i * 128, 128), :] = jnp.zeros((128, 768), F32)
        return carry

    lax.fori_loop(0, 8, clear, 0)
    copies[0].wait()

    def gather_step(k, carry):
        @pl.when(k > 0)
        def _():
            gather_recv(k).wait_recv()

        forward(k).start()
        forward_recv(k).wait_recv()
        return carry

    def product(rows, k):
        where = pl.ds(pl.multiple_of(chip_back(k) * 256, 256), 256)
        return jnp.dot(tile[rows, where], fg[where, :], preferred_element_type=F32)

    def mix_step(k, carry):
        gather_step(k, 0)

        def rows_step(m, inner):
            rows = pl.ds(pl.multiple_of(m * 512, 512), 512)
            acc[rows, :] += product(rows, k)
            return inner

        return lax.fori_loop(0, 2, rows_step, carry)

    lax.fori_loop(0, 7, mix_step, 0)
    gather_step(7, 0)

    def reduce_send(k):
        to = (c + k) % 8
        return remote(send_blocks.at[to], recv_blocks.at[k - 1], rs_s.at[k], rs_r.at[k], (r, to))

    def reduce_step(k, carry):
        to = (c + k) % 8
        rows = pl.ds(pl.multiple_of(to * 128, 128), 128)
        send_blocks[to] = (acc[rows, :] + product(rows, 7)).astype(BF)
        reduce_send(k).start()
        return carry

    lax.fori_loop(1, 8, reduce_step, 0)
    mine = pl.ds(pl.multiple_of(c * 128, 128), 128)
    mixed[...] = acc[mine, :] + product(mine, 7)

    copies[1].wait()
    copies[2].wait()

    @pl.when(moved)
    def _():
        permute().wait_recv()

    def mass_step(k, total):
        mass_send(k).wait_recv()
        return total + recv_mass[k - 1]

    degree = lax.fori_loop(1, 8, mass_step, mass[c])

    def sum_step(k, carry):
        reduce_send(k).wait_recv()
        mixed[...] += recv_blocks[k - 1].astype(F32)
        return carry

    lax.fori_loop(1, 8, sum_step, 0)

    diagonal = lax.broadcasted_iota(jnp.int32, (128, 128), 0) == lax.broadcasted_iota(
        jnp.int32, (128, 128), 1
    )
    column = jnp.sum(jnp.where(diagonal, degree[0:1, :], 0.0), axis=1, keepdims=True)
    inverse = 1.0 / (column + 1.0)
    high = mixed[...].astype(BF)
    low = (mixed[...] - high.astype(F32)).astype(BF)
    mixed_high = x_other
    mixed_high[...] = high
    x_mine[...] = low

    def layer_step(n, carry):
        cols = pl.ds(pl.multiple_of(n * 256, 256), 256)
        aggregate = jnp.dot(mixed_high[...], wn[:, cols], preferred_element_type=F32)
        aggregate += jnp.dot(x_mine[...], wn[:, cols], preferred_element_type=F32)
        own = jnp.dot(own_feat[...], ws[:, cols], preferred_element_type=F32)
        preact = own.astype(BF).astype(F32) + aggregate * inverse + bias[:, cols]
        small = jnp.exp(jnp.minimum(preact, 0.0))
        above = preact > 0
        out_ref[:, cols] = jnp.where(above, preact, small - 1.0).astype(BF)
        grad = cotangent[:, cols].astype(F32) * jnp.where(above, 1.0, small)
        grounded[:, cols] = grad.astype(BF)
        scaled[:, cols] = (grad * inverse).astype(BF)
        bsum[:, cols] = jnp.sum(grad, axis=0, keepdims=True)
        return carry

    lax.fori_loop(0, 4, layer_step, 0)

    lanes = pl.ds(pl.multiple_of(c * 128, 128), 128)
    turned = (((1,), (1,)), ((), ()))
    sgt[:, lanes] = lax.dot_general(
        wn[...], scaled[...], turned, preferred_element_type=F32
    ).astype(BF)

    def spread_send(k):
        return remote(sgt.at[:, lanes], sgt.at[:, lanes], sg_s.at[k], sg_r.at[k], (r, (c + k) % 8))

    def spread_recv(k):
        source = pl.ds(pl.multiple_of(((c + 8 - k) % 8) * 128, 128), 128)
        return remote(sgt.at[:, source], sgt.at[:, source], sg_s.at[k], sg_r.at[k], (r, (c + k) % 8))

    def start_spread(k, carry):
        spread_send(k).start()
        return carry

    lax.fori_loop(1, 8, start_spread, 0)
    tblock[...] = lax.dot_general(
        ws[...], grounded[...], turned, preferred_element_type=F32
    ).astype(BF)

    def self_send():
        return remote(tblock, trecv, t_s.at[0], t_r.at[0], in_dev)

    @pl.when(moved)
    def _():
        self_send().start()

    @pl.when(jnp.logical_not(moved))
    def _():
        trecv[...] = tblock[...]

    @pl.when(core == 0)
    def _():
        x_mine[...] = own_feat[...]
        y_mine[...] = grounded[...]
        y_other[...] = scaled[...]

    @pl.when(core == 1)
    def _():
        x_mine[...] = x_other[...]
        x_other[...] = own_feat[...]
        y_mine[...] = scaled[...]
        y_other[...] = grounded[...]

    flipped = (((0,), (0,)), ((), ()))

    def part(j):
        return pl.ds(j * 256, 256)

    def other_send(j):
        return remote(other.at[part(j)], other_recv.at[part(j)], ot_s.at[j], ot_r.at[j], partner)

    for j in range(3):
        other[part(j), :] = lax.dot_general(
            x_other[:, part(j)], y_other[...], flipped, preferred_element_type=F32
        ).astype(BF)
        other_send(j).start()

    def stage1(j, d):
        axis = axis_orders[j][0]
        rows = pl.ds(pl.multiple_of(j * 256 + ((here[axis] + d) % 4) * 64, 64), 64)
        n = j * 3 + d - 1
        return remote(partial.at[rows], r1.at[n], a1_s.at[n], a1_r.at[n], along(axis, d))

    for j in range(3):
        mine_part = lax.dot_general(
            x_mine[:, part(j)], y_mine[...], flipped, preferred_element_type=F32
        )
        other_send(j).wait_recv()
        partial[part(j), :] = (mine_part + other_recv[part(j), :].astype(F32)).astype(BF)
        for d in range(1, 4):
            stage1(j, d).start()

    bias_slots = (bx, by, bz)

    def bias_send(axis, d):
        n = axis * 3 + d - 1
        slot = bias_slots[axis].at[here[axis]]
        return remote(slot, slot, b_s.at[n], b_r.at[n], along(axis, d))

    def bias_recv(axis, d):
        n = axis * 3 + d - 1
        slot = bias_slots[axis].at[(here[axis] + 4 - d) % 4]
        return remote(slot, slot, b_s.at[n], b_r.at[n], along(axis, d))

    def bias_start(axis, value):
        bias_slots[axis][here[axis]] = value
        for d in range(1, 4):
            bias_send(axis, d).start()

    def bias_total(axis):
        for d in range(1, 4):
            bias_recv(axis, d).wait_recv()
        slots = bias_slots[axis]
        return (slots[0] + slots[1]) + (slots[2] + slots[3])

    bias_start(0, jnp.concatenate([bsum[:, i * 128 : (i + 1) * 128] for i in range(8)], axis=0))

    def wait_spread(k, carry):
        spread_recv(k).wait_recv()
        return carry

    lax.fori_loop(1, 8, wait_spread, 0)

    def pair_send(k):
        return remote(halves.at[k, 1 - core], pair_recv.at[k], pd_s.at[k], pd_r.at[k], partner)

    def row_out(k):
        return remote(
            row_send.at[k], row_recv.at[k - 1], br_s.at[k], br_r.at[k], at_row(chip_fwd(k), core)
        )

    def pair_sum(k):
        pair_send(k).wait_recv()
        return halves[k, core].astype(F32) + pair_recv[k].astype(F32)

    def back_step(t, carry):
        k = (t + 1) % 8
        where = pl.ds(pl.multiple_of(chip_fwd(k) * 256, 256), 256)
        value = jnp.dot(sgt[...], tile[:, where], preferred_element_type=F32)
        halves[k, 0] = value[:, :128].astype(BF)
        halves[k, 1] = value[:, 128:].astype(BF)
        pair_send(k).start()

        @pl.when(t > 0)
        def _():
            row_send[t] = pair_sum(t).astype(BF)
            row_out(t).start()

        return carry

    lax.fori_loop(0, 8, back_step, 0)

    def stage2(j, d):
        axis = axis_orders[j][1]
        rows = pl.ds(pl.multiple_of(((here[axis] + d) % 4) * 16, 16), 16)
        n = j * 3 + d - 1
        return remote(q1.at[j, rows], r2.at[n], a2_s.at[n], a2_r.at[n], along(axis, d))

    def stage3(j, d):
        axis = axis_orders[j][2]
        cols = pl.ds(pl.multiple_of(((here[axis] + d) % 4) * 256, 256), 256)
        n = j * 3 + d - 1
        return remote(q2.at[j, :, cols], r3.at[n], a3_s.at[n], a3_r.at[n], along(axis, d))

    for j in range(3):
        axis = axis_orders[j][0]
        for d in range(1, 4):
            stage1(j, d).wait_recv()
        rows = pl.ds(pl.multiple_of(j * 256 + here[axis] * 64, 64), 64)
        total = partial[rows, :].astype(F32)
        for d in range(3):
            total = total + r1[j * 3 + d].astype(F32)
        q1[j] = total
        for d in range(1, 4):
            stage2(j, d).start()
    bias_start(1, bias_total(0))
    for j in range(3):
        axis = axis_orders[j][1]
        for d in range(1, 4):
            stage2(j, d).wait_recv()
        total = q1[j, pl.ds(pl.multiple_of(here[axis] * 16, 16), 16), :]
        for d in range(3):
            total = total + r2[j * 3 + d]
        q2[j] = total
        for d in range(1, 4):
            stage3(j, d).start()
    bias_start(2, bias_total(1))

    def place(j, shift, axis_step):
        a, b, e = axis_orders[j]
        spot = list(here)
        moving = axis_orders[j][axis_step]
        spot[moving] = (spot[moving] + 4 - shift) % 4
        start = j * 256 + spot[a] * 64
        if axis_step == 0:
            return result.at[pl.ds(pl.multiple_of(start, 64), 64)]
        rows = pl.ds(pl.multiple_of(start + spot[b] * 16, 16), 16)
        if axis_step == 1:
            return result.at[rows]
        return result.at[rows, pl.ds(pl.multiple_of(spot[e] * 256, 256), 256)]

    def back_copy(j, d, axis_step, shift, sends, recvs):
        n = j * 3 + d - 1
        ref = place(j, shift, axis_step)
        return remote(ref, ref, sends.at[n], recvs.at[n], along(axis_orders[j][axis_step], d))

    for j in range(3):
        axis = axis_orders[j][2]
        for d in range(1, 4):
            stage3(j, d).wait_recv()
        cols = pl.ds(pl.multiple_of(here[axis] * 256, 256), 256)
        total = q2[j, :, cols]
        for d in range(3):
            total = total + r3[j * 3 + d]
        place(j, 0, 2)[...] = total.astype(BF)
        for d in range(1, 4):
            back_copy(j, d, 2, 0, g3_s, g3_r).start()
    bias_core = bias_total(2)
    bk[core] = bias_core

    def bias_pair(slot):
        return remote(bk.at[slot], bk.at[slot], b_s.at[9], b_r.at[9], partner)

    bias_pair(core).start()
    for j in range(3):
        for d in range(1, 4):
            back_copy(j, d, 2, d, g3_s, g3_r).wait_recv()
        for d in range(1, 4):
            back_copy(j, d, 1, 0, g2_s, g2_r).start()
    for j in range(3):
        for d in range(1, 4):
            back_copy(j, d, 1, d, g2_s, g2_r).wait_recv()
        for d in range(1, 4):
            back_copy(j, d, 0, 0, g1_s, g1_r).start()

    def finish_copy(j, d, shifted):
        n = j * 4 + d
        axis = axis_orders[j][0]
        spot = (here[axis] + 4 - d) % 4
        rows = pl.ds(pl.multiple_of(j * 256 + spot * 64, 64), 64)
        return remote(result.at[rows], result2.at[rows], fin_s.at[n], fin_r.at[n], partner)

    for j in range(3):
        finish_copy(j, 0, 0).start()

    def row_total(k, total):
        row_out(k).wait_recv()
        return total + row_recv[k - 1].astype(F32)

    @pl.when(moved)
    def _():
        self_send().wait_recv()

    total = pair_sum(0) + trecv[...].astype(F32)
    total = lax.fori_loop(1, 8, row_total, total)
    gin_ref[...] = total.T.astype(BF)

    for j in range(3):
        for d in range(1, 4):
            back_copy(j, d, 0, d, g1_s, g1_r).wait_recv()
            finish_copy(j, d, 0).start()
    bias_pair(1 - core).wait_recv()
    gbias_ref[...] = bk[0] + bk[1]
    for j in range(3):
        for d in range(4):
            finish_copy(j, d, 0).wait_recv()

    @pl.when(core == 0)
    def _():
        gself_ref[...] = result[...]
        gneigh_ref[...] = result2[...]

    @pl.when(core == 1)
    def _():
        gself_ref[...] = result2[...]
        gneigh_ref[...] = result[...]

    def drain(k, carry):
        gather_send(k).wait_send()
        mass_send(k).wait_send()
        reduce_send(k).wait_send()
        spread_send(k).wait_send()
        row_out(k).wait_send()
        return carry

    lax.fori_loop(1, 8, drain, 0)

    def drain_pairs(k, carry):
        forward(k).wait_send()
        pair_send(k).wait_send()
        return carry

    lax.fori_loop(0, 8, drain_pairs, 0)

    @pl.when(moved)
    def _():
        permute().wait_send()
        self_send().wait_send()

    for j in range(3):
        other_send(j).wait_send()
        for d in range(1, 4):
            stage1(j, d).wait_send()
            stage2(j, d).wait_send()
            stage3(j, d).wait_send()
            back_copy(j, d, 2, 0, g3_s, g3_r).wait_send()
            back_copy(j, d, 1, 0, g2_s, g2_r).wait_send()
            back_copy(j, d, 0, 0, g1_s, g1_r).wait_send()
            bias_send(j, d).wait_send()
        for d in range(4):
            finish_copy(j, d, 0).wait_send()
    bias_pair(core).wait_send()


def layer(tile, mass, features, w_neigh, w_self, bias, cotangent):
    vmem = pl.BlockSpec(memory_space=pltpu.VMEM)
    hbm = pl.BlockSpec(memory_space=pl.ANY)
    sem = pltpu.SemaphoreType.DMA
    V = pltpu.VMEM
    shape = jax.ShapeDtypeStruct
    return pl.pallas_call(
        layer_kernel,
        out_shape=(
            shape((128, 1024), BF),
            shape((128, 768), BF),
            shape((768, 1024), BF),
            shape((768, 1024), BF),
            shape((8, 128), F32),
        ),
        in_specs=[hbm, vmem, vmem, hbm, hbm, vmem, vmem],
        out_specs=(vmem,) * 5,
        scratch_shapes=[
            V((1024, 2048), BF), V((768, 1024), BF), V((768, 1024), BF), sem((3,)),
            V((2048, 768), BF), V((1024, 768), F32), V((128, 768), BF), V((8, 128, 768), BF),
            V((7, 128, 768), BF), V((7, 8, 128), F32), V((128, 768), F32),
            V((128, 1024), BF), V((128, 1024), BF), V((768, 1024), BF), V((768, 128), BF), V((768, 128), BF),
            V((128, 768), BF), V((128, 1024), BF), V((128, 768), BF), V((128, 1024), BF),
            V((768, 1024), BF), V((768, 1024), BF), V((768, 1024), BF),
            V((9, 64, 1024), BF), V((3, 64, 1024), F32), V((9, 16, 1024), F32), V((3, 16, 1024), F32),
            V((9, 16, 256), F32), V((768, 1024), BF), V((768, 1024), BF),
            V((8, 2, 768, 128), BF), V((8, 768, 128), BF), V((8, 768, 128), BF), V((7, 768, 128), BF),
            V((1, 1024), F32), V((4, 8, 128), F32), V((4, 8, 128), F32), V((4, 8, 128), F32), V((2, 8, 128), F32),
        ]
        + [sem((8,))] * 4 + [sem((1,))] * 2 + [sem((8,))] * 6 + [sem((1,))] * 2 + [sem((3,))] * 2
        + [sem((9,))] * 12 + [sem((12,))] * 2 + [sem((10,))] * 2 + [sem((8,))] * 4,
        compiler_params=pltpu.CompilerParams(
            collective_id=0, has_side_effects=True, vmem_limit_bytes=58 * 1024 * 1024
        ),
        name="layer",
    )(tile, mass, features, w_neigh, w_self, bias, cotangent)


def local(
    features, w_neigh, w_self, bias, cotangent, block_rows, block_cols, block_vals, block_count
):
    row_size = lax.axis_size("row")
    col_size = lax.axis_size("col")
    node_dev = features.shape[0]
    tile, mass = densify(
        block_vals[0, 0], block_rows[0, 0], block_cols[0, 0], block_count[0], col_size, row_size
    )
    output, grad_input, g_self, g_neigh, g_bias = layer(
        tile, mass, features, w_neigh, w_self, bias.reshape(1, -1), cotangent
    )
    factor = 1.0 / math.sqrt(node_dev * row_size * col_size)
    return (
        output,
        grad_input,
        g_self.astype(F32) * factor,
        g_neigh.astype(F32) * (32.0 * factor),
        g_bias.reshape(-1) * factor,
    )


def solution(mesh):
    in_specs = (
        P(("col", "row"), None),
        P(),
        P(),
        P(),
        P(("row", "col"), None),
        P("row", "col", None),
        P("row", "col", None),
        P("row", "col", None, None, None),
        P("row", "col"),
    )
    out_specs = (P(("row", "col"), None), P(("col", "row"), None), P(), P(), P())
    return jax.shard_map(local, mesh=mesh, in_specs=in_specs, out_specs=out_specs, check_vma=False)
```

time: 458 us -> 166 us (0.36)
  waiting for transfers between devices: 278 us -> 0 us
  Pallas kernels: 3.12 us -> 150 us
  blocking collectives: 99.5 us -> 0 us
  matrix products: 30 us -> 0 us
  between operations: 14.6 us -> 1.3 us
  starting transfers between devices: 7.98 us -> 0 us
    pallas_call x0 -> x1, Pallas kernels: none -> 147 us  [layer(): pl.pallas_call(layer_kernel, out_shape=(shape((128, 1024), BF), shape((12...]
    reduce_scatter x2 -> x0, waiting for transfers between devices: 115 us -> none  [the longest x1 59.1 us: local(): mixed = lax.psum_scatter(part, 'col', scatter_dimension=0, tiled=True)]
    psum x1 -> x0, waiting for transfers between devices: 86.1 us -> none  [local(): lax.psum((part_self, part_neigh, part_bias), ('row', 'col'))]
    psum x1 -> x0, blocking collectives: 79.3 us -> none  [local(): lax.psum((part_self, part_neigh, part_bias), ('row', 'col'))]
    all_gather x2 -> x0, waiting for transfers between devices: 75.7 us -> none  [the longest x1 43.3 us: local(): back_all = lax.all_gather(back_in, 'col', axis=0, tiled=True)]
    dot_general x9 -> x0, matrix products: 30 us -> none  [matmul(): lax.dot_general(a, b, ((contract[0], contract[1]), ((), ())), preferred_e...]
    unnamed x1 -> x0, blocking collectives: 20.2 us -> none
    ppermute x2 -> x0, starting transfers between devices: 7.78 us -> none  [the longest x1 4.62 us: local(): own_feat = lax.ppermute(features, ('row', 'col'), to_out)]
  transfers between devices with their start and end apart: 7 -> 0, of which waited for: 5 -> 0; matrix products, arithmetic and copies ran while one was open for 7% -> 0% of each run, Pallas kernels for 1% -> 0%
where the time goes in v2:
time: 166 us
  Pallas kernels  150 us (90%)
  local copies, waits for them, and re-layouts  7.14 us (4%)
  other arithmetic  6.81 us (4%)
    pallas_call x1, Pallas kernels, layer(): pl.pallas_call(layer_kernel, out_shape=(shape((128, 1024), BF), shape((12...  147 us
    unnamed x16, local copies, waits for them, and re-layouts  7.14 us
    mul x1, other arithmetic, local(): g_neigh.astype(F32) * (32.0 * factor)  5.53 us

profile of v2, /device:TPU:1, one launch (start us, length us, event | category | flops | bytes accessed | tf_op | source)
XLA Modules:
  0.0 165.7 jit_solution(7590729057442590756)
XLA Ops:
  1.3 0.0 copy-start.1
  1.3 1.9 %copy-done.1 = bf16[1,1,96,128,128]{4,3,2,1,0:T(8,128)(2,1)S(1)} copy-done((bf16[1,1,96,128,128]{4,3,2,1,0:T(8,128)(2,1)S(1)}, bf16[1,1,96,128,128]{4,3,2,1,0:T(8,128)(2,1)}, u32[]{:S(2)}) %copy-start.1) | copy-done | bytes 3145752
  3.2 0.0 copy-start.3
  3.2 0.7 copy-done.3
  3.8 0.0 copy-start.4
  3.8 0.7 copy-done.4
  4.5 3.0 %densify.1 = (bf16[1024,2048]{1,0:T(8,128)(2,1)S(1)}, f32[8,8,128]{2,1,0:T(8,128)S(1)}) custom-call(s32[96]{0:T(128)S(1)} %bitcast.9, s32[96]{0:T(128)S(1)} %bitcast.10, s32[1]{0:T(128)} %bitcast.7.count_ref, bf16[96,128,128]{2,1,0:T(8,128)(2,1)S(1)} %bitcast.8), custom_call_target="tpu_custom_call" | custom-call | tf_op jit(solution)/shard_map/densify/pallas_call | solution.py:51
  7.5 0.0 copy-start
  7.5 1.9 %copy-done = bf16[1024,2048]{1,0:T(8,128)(2,1)} copy-done((bf16[1024,2048]{1,0:T(8,128)(2,1)}, bf16[1024,2048]{1,0:T(8,128)(2,1)S(1)}, u32[]{:S(2)}) %copy-start) | copy-done | bytes 4194328
  9.5 0.0 copy-start.2
  9.5 0.6 copy-done.2
  10.1 147.4 %layer.1 = (bf16[128,1024]{1,0:T(8,128)(2,1)}, bf16[128,768]{1,0:T(8,128)(2,1)}, bf16[768,1024]{1,0:T(8,128)(2,1)}, bf16[768,1024]{1,0:T(8,128)(2,1)}, f32[8,128]{1,0:T(8,128)}) custom-call(bf16[1024,2048]{1,0:T(8,128)(2,1)} %copy-done, f32[8,8,128]{2,1,0:T(8,128)} %copy-done.2, bf16[128,768]{1,0:T(8,128)(2,1)} %features.1, bf16[768,1024]{1,0:T(8,128)(2,1)} %wn_hbm.1, ...), custom_call_target="tpu_custom_call" | custom-call | tf_op jit(solution)/shard_map/layer/pallas_call | solution.py:603
  157.5 1.3 multiply_bitcast_fusion
  158.8 0.0 copy-start.5
  158.8 0.0 copy-start.6
  158.8 5.5 %convert_multiply_fusion = (f32[768,1024]{1,0:T(8,128)}, f32[768,1024]{1,0:T(8,128)}) fusion(bf16[768,1024]{1,0:T(8,128)(2,1)} %get-tuple-element.17, bf16[768,1024]{1,0:T(8,128)(2,1)} %get-tuple-element.16), kind=kLoop, calls=%fused_computation | loop fusion | flops 3145728 | bytes 9437184 | tf_op jit(solution)/shard_map/mul | solution.py:652
  164.3 0.0 copy-done.5
  164.4 0.7 copy.17
  165.1 0.0 copy-done.6
  165.1 0.7 copy.18
Async XLA Ops:
  1.3 1.9 %copy-start.1 = (bf16[1,1,96,128,128]{4,3,2,1,0:T(8,128)(2,1)S(1)}, bf16[1,1,96,128,128]{4,3,2,1,0:T(8,128)(2,1)}, u32[]{:S(2)}) copy-start(bf16[1,1,96,128,128]{4,3,2,1,0:T(8,128)(2,1)} %param.16) | copy-start | bytes 9437188
  3.2 0.7 copy-start.3
  3.8 0.7 copy-start.4
  7.5 1.9 %copy-start = (bf16[1024,2048]{1,0:T(8,128)(2,1)}, bf16[1024,2048]{1,0:T(8,128)(2,1)S(1)}, u32[]{:S(2)}) copy-start(bf16[1024,2048]{1,0:T(8,128)(2,1)S(1)} %get-tuple-element.12.tile_hbm) | copy-start | bytes 12582916
  9.5 0.6 copy-start.2
  158.8 5.5 %copy-start.5 = (bf16[128,1024]{1,0:T(8,128)(2,1)S(1)}, bf16[128,1024]{1,0:T(8,128)(2,1)}, u32[]{:S(2)}) copy-start(bf16[128,1024]{1,0:T(8,128)(2,1)} %get-tuple-element.26) | copy-start | bytes 786436
  158.8 6.2 %copy-start.6 = (bf16[128,768]{1,0:T(8,128)(2,1)S(1)}, bf16[128,768]{1,0:T(8,128)(2,1)}, u32[]{:S(2)}) copy-start(bf16[128,768]{1,0:T(8,128)(2,1)} %get-tuple-element.27) | copy-start | bytes 589828

commit v3 on v1

v3 whole, which is shorter than its diff:
```python
import functools
import math

import jax
import jax.numpy as jnp
from jax import lax
from jax.experimental import pallas as pl
from jax.experimental.pallas import tpu as pltpu
from jax.sharding import PartitionSpec as P


def densify_kernel(
    rows_ref, cols_ref, count_ref, vals_hbm, tile_hbm, mass_ref, vals, acc, tile, in_sem, out_sem
):
    row_blocks, col_blocks, size, _ = acc.shape
    pieces = 4
    span = vals.shape[0] // pieces

    def load(q):
        slots = pl.ds(q * span, span)
        return pltpu.make_async_copy(vals_hbm.at[slots], vals.at[slots], in_sem.at[q])

    def store(i):
        rows = pl.ds(pl.multiple_of(i * size, size), size)
        return pltpu.make_async_copy(tile.at[rows], tile_hbm.at[rows], out_sem.at[i])

    for q in range(pieces):
        load(q).start()

    def clear(i, carry):
        for j in range(col_blocks):
            acc[i, j] = jnp.zeros((size, size), jnp.float32)
        return carry

    lax.fori_loop(0, row_blocks, clear, 0)

    def add(s, carry):
        i = rows_ref[s]
        j = cols_ref[s]
        acc[i, j] += vals[s].astype(jnp.float32)
        return carry

    count = count_ref[0]
    for q in range(pieces):
        load(q).wait()
        lax.fori_loop(q * span, jnp.minimum(count, (q + 1) * span), add, 0)
    diagonal = lax.broadcasted_iota(jnp.int32, (size, size), 0) == lax.broadcasted_iota(
        jnp.int32, (size, size), 1
    )

    def finish(i, carry):
        total = jnp.zeros((size, size), jnp.float32)
        start = pl.multiple_of(i * size, size)
        for j in range(col_blocks):
            block = acc[i, j]
            total = total + block
            tile[pl.ds(start, size), j * size : (j + 1) * size] = block.astype(jnp.bfloat16)
        store(i).start()
        sums = jnp.sum(total, axis=1, keepdims=True)
        as_row = jnp.sum(jnp.where(diagonal, sums, 0.0), axis=0, keepdims=True)
        mass_ref[i] = jnp.broadcast_to(as_row, (8, size))
        return carry

    lax.fori_loop(0, row_blocks, finish, 0)
    for i in range(row_blocks):
        store(i).wait()


def densify(values, row_ids, col_ids, live_count, row_blocks, col_blocks):
    slots, size, _ = values.shape
    smem = pl.BlockSpec(memory_space=pltpu.SMEM)
    hbm = pl.BlockSpec(memory_space=pl.ANY)
    vmem = pl.BlockSpec(memory_space=pltpu.VMEM)
    rows, cols = row_blocks * size, col_blocks * size
    return pl.pallas_call(
        densify_kernel,
        out_shape=(
            jax.ShapeDtypeStruct((rows, cols), jnp.bfloat16),
            jax.ShapeDtypeStruct((row_blocks, 8, size), jnp.float32),
        ),
        in_specs=[smem, smem, smem, hbm],
        out_specs=(hbm, vmem),
        scratch_shapes=[
            pltpu.VMEM((slots, size, size), jnp.bfloat16),
            pltpu.VMEM((row_blocks, col_blocks, size, size), jnp.float32),
            pltpu.VMEM((rows, cols), jnp.bfloat16),
            pltpu.SemaphoreType.DMA((4,)),
            pltpu.SemaphoreType.DMA((row_blocks,)),
        ],
        compiler_params=pltpu.CompilerParams(vmem_limit_bytes=60 * 1024 * 1024),
        name="densify",
    )(row_ids, col_ids, live_count, values)


def finish_kernel(
    own_scale, neigh_scale, g_hbm, out_in, gin_in, bias_in,
    own_to, neigh_to, out_to, gin_to, bias_to, held, wide, in_sem, out_sem,
):
    pieces = in_sem.shape[0]
    rows = g_hbm.shape[1]
    step = 2 * rows // pieces
    loads = []
    stores = []
    for p in range(pieces):
        which, at = p % 2, pl.ds(p // 2 * step, step)
        target = (own_to, neigh_to)[which]
        loads.append(pltpu.make_async_copy(g_hbm.at[which, at], held.at[which, at], in_sem.at[p]))
        stores.append(pltpu.make_async_copy(wide.at[which, at], target.at[at], out_sem.at[p]))
    for load in loads:
        load.start()
    out_to[...] = out_in[...]
    gin_to[...] = gin_in[...]
    bias_to[...] = bias_in[...] * own_scale
    for p in range(pieces):
        which, at = p % 2, pl.ds(p // 2 * step, step)
        loads[p].wait()
        wide[which, at] = held[which, at].astype(jnp.float32) * (own_scale, neigh_scale)[which]
        stores[p].start()
    for copy in stores:
        copy.wait()


def finish(grads, output, grad_input, g_bias, own_scale, neigh_scale):
    _, rows, cols = grads.shape
    hbm = pl.BlockSpec(memory_space=pl.ANY)
    vmem = pl.BlockSpec(memory_space=pltpu.VMEM)
    shape = jax.ShapeDtypeStruct
    wide = shape((rows, cols), jnp.float32)
    pieces = 12
    return pl.pallas_call(
        functools.partial(finish_kernel, own_scale, neigh_scale),
        out_shape=(
            wide,
            wide,
            shape(output.shape, output.dtype),
            shape(grad_input.shape, grad_input.dtype),
            shape(g_bias.shape, g_bias.dtype),
        ),
        in_specs=[hbm, vmem, vmem, vmem],
        out_specs=(hbm, hbm, vmem, vmem, vmem),
        scratch_shapes=[
            pltpu.VMEM((2, rows, cols), jnp.bfloat16),
            pltpu.VMEM((2, rows, cols), jnp.float32),
            pltpu.SemaphoreType.DMA((pieces,)),
            pltpu.SemaphoreType.DMA((pieces,)),
        ],
        compiler_params=pltpu.CompilerParams(vmem_limit_bytes=60 * 1024 * 1024),
        name="finish",
    )(grads, output, grad_input, g_bias)


MESH = pl.DeviceIdType.MESH
BF = jnp.bfloat16
F32 = jnp.float32


def remote(src, dst, send, recv, device):
    return pltpu.make_async_remote_copy(
        src_ref=src, dst_ref=dst, send_sem=send, recv_sem=recv, device_id=device, device_id_type=MESH
    )


def layer_kernel(
    tile_hbm, mass, features, wn_hbm, ws_hbm, bias, cotangent,
    out_ref, gin_ref, g_ref, gbias_ref,
    tile, wn, ws, local_sem,
    fg, own_feat, send_blocks, recv_blocks, cross_send, cross_recv,
    mass_recv, mass_cross, mass_sum, mixed, group,
    scaled, grounded, sgt, tblock, trecv,
    x_mine, y_mine, x_other, y_other, other, other_recv, partial,
    r1, q1, r2, q2, r3, result, result2,
    halves, pair_recv, row_send, row_recv, row_group, side_send, side_recv,
    bsum, bx, by, bz, bk,
    gx_s, gx_r, gz_s, gz_r, fw_s, fw_r, pm_s, pm_r, ms_s, ms_r, rs_s, rs_r, rx_s, rx_r,
    sx_s, sx_r, sy_s, sy_r, t_s, t_r,
    ot_s, ot_r, a1_s, a1_r, a2_s, a2_r, a3_s, a3_r, g3_s, g3_r, g2_s, g2_r, g1_s, g1_r, fin_s, fin_r,
    b_s, b_r, pd_s, pd_r, rz_s, rz_r, rl_s, rl_r, w1_sem, w2_sem,
):
    r = lax.axis_index("row")
    c = lax.axis_index("col")
    xl, z, core = r // 8, (r // 2) % 4, r % 2
    y, xh = c // 2, c % 2
    x = xh * 2 + xl

    def device_of(px, py, pz):
        return (((px % 2) * 4 + pz) * 2 + core, py * 2 + px // 2)

    here = (x, y, z)
    axis_orders = ((0, 1, 2), (1, 2, 0), (2, 0, 1))

    def along(axis, d):
        spot = list(here)
        spot[axis] = (spot[axis] + d) % 4
        return device_of(*spot)

    partner = (r + 1 - 2 * core, c)
    here_id = r * 8 + c
    block = r * 8 + c
    first, first_col = block % 16, block // 16

    def target(d):
        from_row = (xl * 4 + (z + 4 - d) % 4) * 2 + core
        node = c * 16 + from_row
        return node // 8, node % 8

    def holder(d):
        chip = first // 8 * 4 + (first // 2 + d) % 4
        return chip * 2 + first % 2, first_col

    def is_here(device):
        return device[0] * 8 + device[1] == here_id

    copies = [
        pltpu.make_async_copy(tile_hbm, tile, local_sem.at[0]),
        pltpu.make_async_copy(ws_hbm, ws, local_sem.at[1]),
        pltpu.make_async_copy(wn_hbm, wn, local_sem.at[2]),
    ]
    for copy in copies:
        copy.start()

    barrier = pltpu.get_barrier_semaphore()

    def hello(device):
        pl.semaphore_signal(barrier, inc=1, device_id=device, device_id_type=MESH)

    x_side = (((1 - xl) * 4 + z) * 2 + core, c)
    far_side = (r, y * 2 + 1 - xh)

    def z_peer(d):
        return ((xl * 4 + (z + d) % 4) * 2 + core, c)

    def y_peer(d):
        return (r, ((y + d) % 4) * 2 + xh)

    for d in range(1, 4):
        hello(z_peer(d))
        hello(y_peer(d))
    hello(x_side)
    hello(far_side)
    hello(partner)
    hello((((1 - xl) * 4 + z) * 2 + core, y * 2 + 1 - xh))

    remote_peers = 10
    for d in range(4):
        for device in (target(d), holder(d)):
            away = jnp.logical_not(is_here(device))
            remote_peers = remote_peers + away.astype(jnp.int32)

            @pl.when(away)
            def _():
                hello(device)

    pl.semaphore_wait(barrier, remote_peers)

    for n in range(3):
        fg[n, pl.ds(r * 128, 128), :] = features[:, n * 256 : (n + 1) * 256]

    def source_rows_start(s, d, k):
        chip = ((xl + s) % 2) * 4 + (z + 4 - d) % 4
        return (chip * 2 + k) * 128

    def source_rows(s, d, k):
        return pl.ds(pl.multiple_of(source_rows_start(s, d, k), 128), 128)

    def side_gather(n):
        ref = fg.at[n, source_rows(0, 0, core)]
        return remote(ref, ref, gx_s.at[n], gx_r.at[n], x_side)

    def gather_send(n, s, d):
        m = (n * 2 + s) * 4 + d
        ref = fg.at[n, source_rows(s, 0, core)]
        return remote(ref, ref, gz_s.at[m], gz_r.at[m], z_peer(d))

    def gather_recv(n, s, d):
        m = (n * 2 + s) * 4 + d
        ref = fg.at[n, source_rows(s, d, core)]
        return remote(ref, ref, gz_s.at[m], gz_r.at[m], z_peer(d))

    def forward(n, s, d):
        m = (n * 2 + s) * 4 + d
        ref = fg.at[n, source_rows(s, d, core)]
        return remote(ref, ref, fw_s.at[m], fw_r.at[m], partner)

    def own_piece(n, d):
        return own_feat.at[n, pl.ds(d * 32, 32)]

    def permute(n, d):
        start = source_rows_start(0, d, core) + d * 32
        rows = pl.ds(pl.multiple_of(start, 32), 32)
        m = d * 3 + n
        return remote(fg.at[n, rows], own_piece(n, d), pm_s.at[m], pm_r.at[m], target(d))

    def permute_start(n):
        for d in range(4):

            @pl.when(jnp.logical_not(is_here(target(d))))
            def _():
                permute(n, d).start()

            @pl.when(is_here(target(d)))
            def _():
                start = source_rows_start(0, d, core) + d * 32
                own_feat[n, d * 32 : (d + 1) * 32, :] = fg[n, pl.ds(pl.multiple_of(start, 32), 32), :]

    def permute_wait(n):
        for d in range(4):

            @pl.when(jnp.logical_not(is_here(holder(d))))
            def _():
                permute(n, d).wait_recv()

    def mass_send(d):
        to = ((y + d) % 4) * 2
        return remote(mass.at[pl.ds(to, 2)], mass_recv.at[d - 1], ms_s.at[d], ms_r.at[d], y_peer(d))

    def mass_side():
        return remote(mass_sum.at[1 - xh], mass_cross, ms_s.at[0], ms_r.at[0], far_side)

    def spread_gather(n):
        side_gather(n).wait_recv()
        for s in range(2):
            for d in range(1, 4):
                gather_send(n, s, d).start()

    for n in range(3):
        side_gather(n).start()
    for d in range(1, 4):
        gather_send(0, 0, d).start()
    for d in range(1, 4):
        mass_send(d).start()
    side_gather(0).wait_recv()
    for d in range(1, 4):
        gather_send(0, 1, d).start()
    spread_gather(1)

    copies[0].wait()

    def reduce_send(n, d):
        m = n * 4 + d
        return remote(
            send_blocks.at[n, d], recv_blocks.at[n, d - 1], rs_s.at[m], rs_r.at[m], y_peer(d)
        )

    def cross(n):
        return remote(cross_send.at[n], cross_recv.at[n], rx_s.at[n], rx_r.at[n], far_side)

    def mix(n):
        for s in range(2):
            forward(n, s, 0).start()
        for s in range(2):
            for d in range(1, 4):
                gather_recv(n, s, d).wait_recv()
                forward(n, s, d).start()
        if n == 0:
            spread_gather(2)
        for s in range(2):
            for d in range(4):
                forward(n, s, d).wait_recv()

        def mix_step(t, carry):
            d = (t + 1) % 4
            rows = pl.ds(pl.multiple_of(((y + d) % 4) * 256, 256), 256)
            value = jnp.dot(tile[rows, :], fg[n], preferred_element_type=F32)

            @pl.when(t < 3)
            def _():
                send_blocks[n, d] = value.astype(BF)
                reduce_send(n, d).start()

            @pl.when(t == 3)
            def _():
                group[n, 0] = value[:128]
                group[n, 1] = value[128:]

            return carry

        lax.fori_loop(0, 4, mix_step, 0)

    def cross_start(n):
        for d in range(1, 4):
            reduce_send(n, d).wait_recv()
        for h in range(2):
            total = group[n, h]
            for d in range(3):
                total = total + recv_blocks[n, d, h * 128 : (h + 1) * 128].astype(F32)
            group[n, h] = total
        cross_send[n] = group[n, 1 - xh].astype(BF)
        cross(n).start()

    mix(0)
    permute_start(0)
    mix(1)
    permute_start(1)
    cross_start(0)
    for d in range(1, 4):
        mass_send(d).wait_recv()
    for h in range(2):
        mass_sum[h] = mass[y * 2 + h] + ((mass_recv[0, h] + mass_recv[1, h]) + mass_recv[2, h])
    mass_side().start()
    mix(2)
    permute_start(2)
    cross_start(1)
    cross_start(2)
    copies[1].wait()
    copies[2].wait()

    for n in range(3):
        permute_wait(n)
    mass_side().wait_recv()
    degree = mass_sum[xh] + mass_cross[...]
    for n in range(3):
        cross(n).wait_recv()
        mixed[:, n * 256 : (n + 1) * 256] = group[n, xh] + cross_recv[n].astype(F32)

    diagonal = lax.broadcasted_iota(jnp.int32, (128, 128), 0) == lax.broadcasted_iota(
        jnp.int32, (128, 128), 1
    )
    column = jnp.sum(jnp.where(diagonal, degree[0:1, :], 0.0), axis=1, keepdims=True)
    inverse = 1.0 / (column + 1.0)
    high = mixed[...].astype(BF)
    low = (mixed[...] - high.astype(F32)).astype(BF)
    mixed_high = x_other
    mixed_high[...] = high
    x_mine[...] = low

    def layer_step(n, carry):
        cols = pl.ds(pl.multiple_of(n * 256, 256), 256)
        aggregate = jnp.dot(mixed_high[...], wn[:, cols], preferred_element_type=F32)
        aggregate += jnp.dot(x_mine[...], wn[:, cols], preferred_element_type=F32)
        own = jnp.dot(own_feat[0], ws[0:256, cols], preferred_element_type=F32)
        own += jnp.dot(own_feat[1], ws[256:512, cols], preferred_element_type=F32)
        own += jnp.dot(own_feat[2], ws[512:768, cols], preferred_element_type=F32)
        preact = own.astype(BF).astype(F32) + aggregate * inverse + bias[:, cols]
        small = jnp.exp(jnp.minimum(preact, 0.0))
        above = preact > 0
        out_ref[:, cols] = jnp.where(above, preact, small - 1.0).astype(BF)
        grad = cotangent[:, cols].astype(F32) * jnp.where(above, 1.0, small)
        grounded[:, cols] = grad.astype(BF)
        scaled[:, cols] = (grad * inverse).astype(BF)
        bsum[:, cols] = jnp.sum(grad, axis=0, keepdims=True)
        return carry

    lax.fori_loop(0, 4, layer_step, 0)

    lanes = pl.ds(pl.multiple_of(c * 128, 128), 128)
    turned = (((1,), (1,)), ((), ()))

    def spread_ref(n, s, d):
        who = ((y + 4 - d) % 4) * 2 + (xh + s) % 2
        return sgt.at[pl.ds(n * 256, 256), pl.ds(pl.multiple_of(who * 128, 128), 128)]

    def spread_side(n):
        ref = spread_ref(n, 0, 0)
        return remote(ref, ref, sx_s.at[n], sx_r.at[n], far_side)

    def spread_send(n, s, d):
        m = (n * 2 + s) * 4 + d
        ref = spread_ref(n, s, 0)
        return remote(ref, ref, sy_s.at[m], sy_r.at[m], y_peer(d))

    def spread_recv(n, s, d):
        m = (n * 2 + s) * 4 + d
        ref = spread_ref(n, s, d)
        return remote(ref, ref, sy_s.at[m], sy_r.at[m], y_peer(d))

    def spread_more(n, sides):
        for s in sides:
            if s == 1:
                spread_side(n).wait_recv()
            for d in range(1, 4):
                spread_send(n, s, d).start()

    for n in range(3):
        part_rows = pl.ds(n * 256, 256)
        sgt[part_rows, lanes] = lax.dot_general(
            wn[part_rows, :], scaled[...], turned, preferred_element_type=F32
        ).astype(BF)
        spread_side(n).start()
        if n == 0:
            spread_more(0, (0,))
    for n in range(3):
        part_rows = pl.ds(n * 256, 256)
        value = lax.dot_general(
            ws[part_rows, :], grounded[...], turned, preferred_element_type=F32
        ).astype(BF)
        for d in range(4):
            tblock[d, n] = value[d * 64 : (d + 1) * 64]

    def self_send(d):
        return remote(tblock.at[d], trecv.at[d], t_s.at[d], t_r.at[d], holder(d))

    for d in range(4):

        @pl.when(jnp.logical_not(is_here(holder(d))))
        def _():
            self_send(d).start()

        @pl.when(is_here(holder(d)))
        def _():
            trecv[d] = tblock[d]

    def self_wait():
        for d in range(4):

            @pl.when(jnp.logical_not(is_here(target(d))))
            def _():
                self_send(d).wait_recv()

    flipped = (((0,), (0,)), ((), ()))

    def part(j):
        return pl.ds(j * 256, 256)

    def other_send(j):
        return remote(other.at[part(j)], other_recv.at[part(j)], ot_s.at[j], ot_r.at[j], partner)

    def ar_other():
        @pl.when(core == 0)
        def _():
            for n in range(3):
                x_mine[:, n * 256 : (n + 1) * 256] = own_feat[n]
            y_mine[...] = grounded[...]
            y_other[...] = scaled[...]

        @pl.when(core == 1)
        def _():
            x_mine[...] = x_other[...]
            for n in range(3):
                x_other[:, n * 256 : (n + 1) * 256] = own_feat[n]
            y_mine[...] = scaled[...]
            y_other[...] = grounded[...]

        for j in range(3):
            other[part(j), :] = lax.dot_general(
                x_other[:, part(j)], y_other[...], flipped, preferred_element_type=F32
            ).astype(BF)
            other_send(j).start()

    def stage1(j, d):
        axis = axis_orders[j][0]
        rows = pl.ds(pl.multiple_of(j * 256 + ((here[axis] + d) % 4) * 64, 64), 64)
        n = j * 3 + d - 1
        return remote(partial.at[rows], r1.at[n], a1_s.at[n], a1_r.at[n], along(axis, d))

    bias_slots = (bx, by, bz)

    def bias_send(axis, d):
        n = axis * 3 + d - 1
        slot = bias_slots[axis].at[here[axis]]
        return remote(slot, slot, b_s.at[n], b_r.at[n], along(axis, d))

    def bias_recv(axis, d):
        n = axis * 3 + d - 1
        slot = bias_slots[axis].at[(here[axis] + 4 - d) % 4]
        return remote(slot, slot, b_s.at[n], b_r.at[n], along(axis, d))

    def bias_start(axis, value):
        bias_slots[axis][here[axis]] = value
        for d in range(1, 4):
            bias_send(axis, d).start()

    def bias_total(axis):
        for d in range(1, 4):
            bias_recv(axis, d).wait_recv()
        slots = bias_slots[axis]
        return (slots[0] + slots[1]) + (slots[2] + slots[3])

    def ar_mine():
        for j in range(3):
            mine_part = lax.dot_general(
                x_mine[:, part(j)], y_mine[...], flipped, preferred_element_type=F32
            )
            other_send(j).wait_recv()
            partial[part(j), :] = (mine_part + other_recv[part(j), :].astype(F32)).astype(BF)
            for d in range(1, 4):
                stage1(j, d).start()

        bias_start(0, jnp.concatenate([bsum[:, i * 128 : (i + 1) * 128] for i in range(8)], axis=0))

    def pair_send(n, d):
        m = n * 4 + d
        return remote(halves.at[n, d, 1 - core], pair_recv.at[n, d], pd_s.at[m], pd_r.at[m], partner)

    def row_out(n, d):
        m = n * 4 + d
        return remote(row_send.at[n, d], row_recv.at[n, d - 1], rz_s.at[m], rz_r.at[m], z_peer(d))

    def row_side(n):
        return remote(side_send.at[n], side_recv.at[n], rl_s.at[n], rl_r.at[n], x_side)

    def pair_sum(n, d):
        pair_send(n, d).wait_recv()
        row_group[n] = halves[n, d, core].astype(F32) + pair_recv[n, d].astype(F32)
        q = (4 - d) % 4
        rows = pl.ds(pl.multiple_of(q * 64, 64), 64)
        row_group[n, xl, rows, :] = row_group[n, xl, rows, :] + trecv[q, n].astype(F32)
        return row_group[n]

    def back(n):
        for s in range(2):
            for d in range(1, 4):
                spread_recv(n, s, d).wait_recv()

        def back_step(t, carry):
            d = (t + 1) % 4
            for side in range(2):
                chip = side * 4 + (z + d) % 4
                where = pl.ds(pl.multiple_of(chip * 256, 256), 256)
                value = jnp.dot(
                    sgt[n * 256 : (n + 1) * 256, :], tile[:, where], preferred_element_type=F32
                )
                halves[n, d, 0, side] = value[:, :128].astype(BF)
                halves[n, d, 1, side] = value[:, 128:].astype(BF)
            pair_send(n, d).start()

            @pl.when(t > 0)
            def _():
                row_send[n, t] = pair_sum(n, t).astype(BF)
                row_out(n, t).start()

            return carry

        lax.fori_loop(0, 4, back_step, 0)
        pair_sum(n, 0)

    def row_cross(n):
        for d in range(1, 4):
            row_out(n, d).wait_recv()
        total = row_group[n]
        for d in range(3):
            total = total + row_recv[n, d].astype(F32)
        row_group[n] = total
        side_send[n] = row_group[n, 1 - xl].astype(BF)
        row_side(n).start()

    def row_finish(n):
        rows = slice(n * 256, (n + 1) * 256)
        row_side(n).wait_recv()
        total = row_group[n, xl] + side_recv[n].astype(F32)
        gin_ref[:, rows] = total.T.astype(BF)

    def stage2(j, d):
        axis = axis_orders[j][1]
        rows = pl.ds(pl.multiple_of(((here[axis] + d) % 4) * 16, 16), 16)
        n = j * 3 + d - 1
        return remote(q1.at[j, rows], r2.at[n], a2_s.at[n], a2_r.at[n], along(axis, d))

    def stage3(j, d):
        axis = axis_orders[j][2]
        cols = pl.ds(pl.multiple_of(((here[axis] + d) % 4) * 256, 256), 256)
        n = j * 3 + d - 1
        return remote(q2.at[j, :, cols], r3.at[n], a3_s.at[n], a3_r.at[n], along(axis, d))

    def ar_sum1():
        for j in range(3):
            axis = axis_orders[j][0]
            for d in range(1, 4):
                stage1(j, d).wait_recv()
            rows = pl.ds(pl.multiple_of(j * 256 + here[axis] * 64, 64), 64)
            total = partial[rows, :].astype(F32)
            for d in range(3):
                total = total + r1[j * 3 + d].astype(F32)
            q1[j] = total
            for d in range(1, 4):
                stage2(j, d).start()
        bias_start(1, bias_total(0))

    def ar_sum2():
        for j in range(3):
            axis = axis_orders[j][1]
            for d in range(1, 4):
                stage2(j, d).wait_recv()
            total = q1[j, pl.ds(pl.multiple_of(here[axis] * 16, 16), 16), :]
            for d in range(3):
                total = total + r2[j * 3 + d]
            q2[j] = total
            for d in range(1, 4):
                stage3(j, d).start()
        bias_start(2, bias_total(1))

    def place(j, shift, axis_step):
        a, b, e = axis_orders[j]
        spot = list(here)
        moving = axis_orders[j][axis_step]
        spot[moving] = (spot[moving] + 4 - shift) % 4
        start = j * 256 + spot[a] * 64
        if axis_step == 0:
            return result.at[pl.ds(pl.multiple_of(start, 64), 64)]
        rows = pl.ds(pl.multiple_of(start + spot[b] * 16, 16), 16)
        if axis_step == 1:
            return result.at[rows]
        return result.at[rows, pl.ds(pl.multiple_of(spot[e] * 256, 256), 256)]

    def back_copy(j, d, axis_step, shift, sends, recvs):
        n = j * 3 + d - 1
        ref = place(j, shift, axis_step)
        return remote(ref, ref, sends.at[n], recvs.at[n], along(axis_orders[j][axis_step], d))

    def bias_pair(slot):
        return remote(bk.at[slot], bk.at[slot], b_s.at[9], b_r.at[9], partner)

    def ar_sum3():
        for j in range(3):
            axis = axis_orders[j][2]
            for d in range(1, 4):
                stage3(j, d).wait_recv()
            cols = pl.ds(pl.multiple_of(here[axis] * 256, 256), 256)
            total = q2[j, :, cols]
            for d in range(3):
                total = total + r3[j * 3 + d]
            place(j, 0, 2)[...] = total.astype(BF)
            for d in range(1, 4):
                back_copy(j, d, 2, 0, g3_s, g3_r).start()
        bias_core = bias_total(2)
        bk[core] = bias_core

        bias_pair(core).start()

    def ar_gather2():
        for j in range(3):
            for d in range(1, 4):
                back_copy(j, d, 2, d, g3_s, g3_r).wait_recv()
            for d in range(1, 4):
                back_copy(j, d, 1, 0, g2_s, g2_r).start()

    def ar_gather1():
        for j in range(3):
            for d in range(1, 4):
                back_copy(j, d, 1, d, g2_s, g2_r).wait_recv()
            for d in range(1, 4):
                back_copy(j, d, 0, 0, g1_s, g1_r).start()

    def finish_rows(j, d):
        spot = (here[axis_orders[j][0]] + 4 - d) % 4
        return pl.ds(pl.multiple_of(j * 256 + spot * 64, 64), 64)

    def finish_copy(j, d):
        n = j * 4 + d
        rows = finish_rows(j, d)
        return remote(result.at[rows], result2.at[rows], fin_s.at[n], fin_r.at[n], partner)

    def own_out(j, d):
        ref = result.at[finish_rows(j, d)]
        return pltpu.make_async_copy(ref, g_ref.at[core, finish_rows(j, d)], w1_sem.at[j * 4 + d])

    def pair_out(j, d):
        ref = result2.at[finish_rows(j, d)]
        return pltpu.make_async_copy(
            ref, g_ref.at[1 - core, finish_rows(j, d)], w2_sem.at[j * 4 + d]
        )

    def ar_hand():
        for j in range(3):
            finish_copy(j, 0).start()
            own_out(j, 0).start()

    def ar_finish():
        for j in range(3):
            for d in range(1, 4):
                back_copy(j, d, 0, d, g1_s, g1_r).wait_recv()
                finish_copy(j, d).start()
                own_out(j, d).start()
        bias_pair(1 - core).wait_recv()
        total = bk[0] + bk[1]
        gbias_ref[...] = jnp.concatenate([total[i : i + 1, :] for i in range(8)], axis=1)
        for j in range(3):
            for d in range(4):
                finish_copy(j, d).wait_recv()
                pair_out(j, d).start()

    spread_more(0, (1,))
    spread_more(1, (0, 1))
    ar_other()
    spread_more(2, (0, 1))
    ar_mine()
    self_wait()
    back(0)
    back(1)
    ar_sum1()
    back(2)
    row_cross(0)
    ar_sum2()
    row_cross(1)
    ar_sum3()
    row_cross(2)
    ar_gather2()
    ar_gather1()
    ar_hand()

    for n in range(3):
        row_finish(n)
    ar_finish()

    for d in range(4):

        @pl.when(jnp.logical_not(is_here(target(d))))
        def _():
            for n in range(3):
                permute(n, d).wait_send()

        @pl.when(jnp.logical_not(is_here(holder(d))))
        def _():
            self_send(d).wait_send()

    def drain_forward():
        for n in range(3):
            side_gather(n).wait_send()
            cross(n).wait_send()
            for d in range(1, 4):
                reduce_send(n, d).wait_send()
            for s in range(2):
                for d in range(1, 4):
                    gather_send(n, s, d).wait_send()
                for d in range(4):
                    forward(n, s, d).wait_send()
        for d in range(1, 4):
            mass_send(d).wait_send()
        mass_side().wait_send()

    def drain_back():
        for n in range(3):
            spread_side(n).wait_send()
            row_side(n).wait_send()
            for d in range(4):
                pair_send(n, d).wait_send()
            for d in range(1, 4):
                row_out(n, d).wait_send()
                for s in range(2):
                    spread_send(n, s, d).wait_send()

    def drain_ar():
        for j in range(3):
            other_send(j).wait_send()
            for d in range(1, 4):
                stage1(j, d).wait_send()
                stage2(j, d).wait_send()
                stage3(j, d).wait_send()
                back_copy(j, d, 2, 0, g3_s, g3_r).wait_send()
                back_copy(j, d, 1, 0, g2_s, g2_r).wait_send()
                back_copy(j, d, 0, 0, g1_s, g1_r).wait_send()
                bias_send(j, d).wait_send()
            for d in range(4):
                finish_copy(j, d).wait_send()
                own_out(j, d).wait()
                pair_out(j, d).wait()
        bias_pair(core).wait_send()

    drain_forward()
    drain_back()
    drain_ar()


def layer(tile, mass, features, w_neigh, w_self, bias, cotangent):
    vmem = pl.BlockSpec(memory_space=pltpu.VMEM)
    hbm = pl.BlockSpec(memory_space=pl.ANY)
    sem = pltpu.SemaphoreType.DMA
    V = pltpu.VMEM
    shape = jax.ShapeDtypeStruct
    return pl.pallas_call(
        layer_kernel,
        out_shape=(
            shape((128, 1024), BF),
            shape((128, 768), BF),
            shape((2, 768, 1024), BF),
            shape((1, 1024), F32),
        ),
        in_specs=[hbm, vmem, vmem, hbm, hbm, vmem, vmem],
        out_specs=(vmem, vmem, hbm, vmem),
        scratch_shapes=[
            V((1024, 2048), BF), V((768, 1024), BF), V((768, 1024), BF), sem((3,)),
            V((3, 2048, 256), BF), V((3, 128, 256), BF), V((3, 4, 256, 256), BF),
            V((3, 3, 256, 256), BF), V((3, 128, 256), BF), V((3, 128, 256), BF),
            V((3, 2, 8, 128), F32), V((8, 128), F32), V((2, 8, 128), F32), V((128, 768), F32),
            V((3, 2, 128, 256), F32),
            V((128, 1024), BF), V((128, 1024), BF), V((768, 1024), BF), V((4, 3, 64, 128), BF), V((4, 3, 64, 128), BF),
            V((128, 768), BF), V((128, 1024), BF), V((128, 768), BF), V((128, 1024), BF),
            V((768, 1024), BF), V((768, 1024), BF), V((768, 1024), BF),
            V((9, 64, 1024), BF), V((3, 64, 1024), F32), V((9, 16, 1024), F32), V((3, 16, 1024), F32),
            V((9, 16, 256), F32), V((768, 1024), BF), V((768, 1024), BF),
            V((3, 4, 2, 2, 256, 128), BF), V((3, 4, 2, 256, 128), BF), V((3, 4, 2, 256, 128), BF),
            V((3, 3, 2, 256, 128), BF), V((3, 2, 256, 128), F32), V((3, 256, 128), BF), V((3, 256, 128), BF),
            V((1, 1024), F32), V((4, 8, 128), F32), V((4, 8, 128), F32), V((4, 8, 128), F32), V((2, 8, 128), F32),
        ]
        + [sem((3,))] * 2 + [sem((24,))] * 4 + [sem((12,))] * 2 + [sem((4,))] * 2 + [sem((12,))] * 2
        + [sem((3,))] * 4 + [sem((24,))] * 2 + [sem((4,))] * 2 + [sem((3,))] * 2
        + [sem((9,))] * 12 + [sem((12,))] * 2 + [sem((10,))] * 2 + [sem((12,))] * 4 + [sem((3,))] * 2
        + [sem((12,))] * 2,
        compiler_params=pltpu.CompilerParams(
            collective_id=0, has_side_effects=True, vmem_limit_bytes=58 * 1024 * 1024
        ),
        name="layer",
    )(tile, mass, features, w_neigh, w_self, bias, cotangent)


def local(
    features, w_neigh, w_self, bias, cotangent, block_rows, block_cols, block_vals, block_count
):
    row_size = lax.axis_size("row")
    col_size = lax.axis_size("col")
    node_dev = features.shape[0]
    tile, mass = densify(
        block_vals[0, 0], block_rows[0, 0], block_cols[0, 0], block_count[0], col_size, row_size
    )
    output, grad_input, grads, g_bias = layer(
        tile, mass, features, w_neigh, w_self, bias.reshape(1, -1), cotangent
    )
    factor = 1.0 / math.sqrt(node_dev * row_size * col_size)
    grad_self, grad_neigh, output, grad_input, g_bias = finish(
        grads, output, grad_input, g_bias, factor, 32.0 * factor
    )
    return output, grad_input, grad_self, grad_neigh, g_bias.reshape(-1)


def solution(mesh):
    in_specs = (
        P(("col", "row"), None),
        P(),
        P(),
        P(),
        P(("row", "col"), None),
        P("row", "col", None),
        P("row", "col", None),
        P("row", "col", None, None, None),
        P("row", "col"),
    )
    out_specs = (P(("row", "col"), None), P(("col", "row"), None), P(), P(), P())
    return jax.shard_map(local, mesh=mesh, in_specs=in_specs, out_specs=out_specs, check_vma=False)
```

time: 458 us -> 133 us (0.29)
  waiting for transfers between devices: 278 us -> 0 us
  Pallas kernels: 3.12 us -> 131 us
  blocking collectives: 99.5 us -> 0 us
  matrix products: 30 us -> 0 us
  between operations: 14.6 us -> 1.29 us
  other arithmetic: 10.8 us -> 0 us
  local copies, waits for them, and re-layouts: 10.2 us -> 0 us
  starting transfers between devices: 7.98 us -> 0 us
    pallas_call x1 -> x3, Pallas kernels: 3.12 us -> 131 us  [the longest x1 120 us: layer(): pl.pallas_call(layer_kernel, out_shape=(shape((128, 1024), BF), shape((12...]
    reduce_scatter x2 -> x0, waiting for transfers between devices: 115 us -> none  [the longest x1 59.1 us: local(): mixed = lax.psum_scatter(part, 'col', scatter_dimension=0, tiled=True)]
    psum x1 -> x0, waiting for transfers between devices: 86.1 us -> none  [local(): lax.psum((part_self, part_neigh, part_bias), ('row', 'col'))]
    psum x1 -> x0, blocking collectives: 79.3 us -> none  [local(): lax.psum((part_self, part_neigh, part_bias), ('row', 'col'))]
    all_gather x2 -> x0, waiting for transfers between devices: 75.7 us -> none  [the longest x1 43.3 us: local(): back_all = lax.all_gather(back_in, 'col', axis=0, tiled=True)]
    dot_general x9 -> x0, matrix products: 30 us -> none  [matmul(): lax.dot_general(a, b, ((contract[0], contract[1]), ((), ())), preferred_e...]
    unnamed x1 -> x0, blocking collectives: 20.2 us -> none
    unnamed x26 -> x0, local copies, waits for them, and re-layouts: 10.2 us -> none
  transfers between devices with their start and end apart: 7 -> 0, of which waited for: 5 -> 0; matrix products, arithmetic and copies ran while one was open for 7% -> 0% of each run, Pallas kernels for 1% -> 0%
where the time goes in v3:
time: 133 us
  Pallas kernels  131 us (98%)
    pallas_call x1, Pallas kernels, layer(): pl.pallas_call(layer_kernel, out_shape=(shape((128, 1024), BF), shape((12...  120 us
    pallas_call x1, Pallas kernels, finish(): pl.pallas_call(functools.partial(finish_kernel, own_scale, neigh_scale),...  5.67 us
    pallas_call x1, Pallas kernels, densify(): pl.pallas_call(densify_kernel, out_shape=(jax.ShapeDtypeStruct((rows, col...  5.55 us

profile of v3, /device:TPU:1, one launch (start us, length us, event | category | flops | bytes accessed | tf_op | source)
XLA Modules:
  0.0 132.6 jit_solution(333253106156366785)
XLA Ops:
  1.3 5.5 %densify.1 = (bf16[1024,2048]{1,0:T(8,128)(2,1)}, f32[8,8,128]{2,1,0:T(8,128)}) custom-call(s32[96]{0:T(128)} %bitcast.9, s32[96]{0:T(128)} %bitcast.10, s32[1]{0:T(128)} %bitcast.6.count_ref, bf16[96,128,128]{2,1,0:T(8,128)(2,1)} %bitcast.7), custom_call_target="tpu_custom_call" | custom-call | tf_op jit(solution)/shard_map/densify/pallas_call | solution.py:75
  6.8 120.0 %layer.1 = (bf16[128,1024]{1,0:T(8,128)(2,1)}, bf16[128,768]{1,0:T(8,128)(2,1)}, bf16[2,768,1024]{2,1,0:T(8,128)(2,1)}, f32[1,1024]{1,0:T(1,128)}) custom-call(bf16[1024,2048]{1,0:T(8,128)(2,1)} %get-tuple-element.16.tile_hbm, f32[8,8,128]{2,1,0:T(8,128)} %get-tuple-element.17.mass, bf16[128,768]{1,0:T(8,128)(2,1)} %features.1, bf16[768,1024]{1,0:T(8,128)(2,1)} %wn_hbm.1, ...), custom_call_target="tpu_custom_call" | custom-call | tf_op jit(solution)/shard_map/layer/pallas_call | solution.py:859
  126.9 5.7 %finish.1 = (f32[768,1024]{1,0:T(8,128)}, f32[768,1024]{1,0:T(8,128)}, bf16[128,1024]{1,0:T(8,128)(2,1)}, bf16[128,768]{1,0:T(8,128)(2,1)}, f32[1,1024]{1,0:T(1,128)}) custom-call(bf16[2,768,1024]{2,1,0:T(8,128)(2,1)} %get-tuple-element.18.g_hbm, bf16[128,1024]{1,0:T(8,128)(2,1)} %get-tuple-element.19.out_in, bf16[128,768]{1,0:T(8,128)(2,1)} %get-tuple-element.20.gin_in, ...), custom_call_target="tpu_custom_call" | custom-call | tf_op jit(solution)/shard_map/finish/pallas_call | solution.py:130

commit v4 on v3

--- a/solution.py
+++ b/solution.py
@@ -10,7 +10,8 @@
 
 
 def densify_kernel(
-    rows_ref, cols_ref, count_ref, vals_hbm, tile_hbm, mass_ref, vals, acc, tile, in_sem, out_sem
+    rows_hbm, cols_hbm, count_hbm, vals_hbm, tile, mass_ref,
+    rows_ref, cols_ref, count_ref, vals, acc, in_sem, id_sem,
 ):
     row_blocks, col_blocks, size, _ = acc.shape
     pieces = 4
@@ -20,10 +21,13 @@
         slots = pl.ds(q * span, span)
         return pltpu.make_async_copy(vals_hbm.at[slots], vals.at[slots], in_sem.at[q])
 
-    def store(i):
-        rows = pl.ds(pl.multiple_of(i * size, size), size)
-        return pltpu.make_async_copy(tile.at[rows], tile_hbm.at[rows], out_sem.at[i])
-
+    ids = [
+        pltpu.make_async_copy(rows_hbm, rows_ref, id_sem.at[0]),
+        pltpu.make_async_copy(cols_hbm, cols_ref, id_sem.at[1]),
+        pltpu.make_async_copy(count_hbm, count_ref, id_sem.at[2]),
+    ]
+    for copy in ids:
+        copy.start()
     for q in range(pieces):
         load(q).start()
 
@@ -40,6 +44,8 @@
         acc[i, j] += vals[s].astype(jnp.float32)
         return carry
 
+    for copy in ids:
+        copy.wait()
     count = count_ref[0]
     for q in range(pieces):
         load(q).wait()
@@ -55,21 +61,17 @@
             block = acc[i, j]
             total = total + block
             tile[pl.ds(start, size), j * size : (j + 1) * size] = block.astype(jnp.bfloat16)
-        store(i).start()
         sums = jnp.sum(total, axis=1, keepdims=True)
         as_row = jnp.sum(jnp.where(diagonal, sums, 0.0), axis=0, keepdims=True)
         mass_ref[i] = jnp.broadcast_to(as_row, (8, size))
         return carry
 
     lax.fori_loop(0, row_blocks, finish, 0)
-    for i in range(row_blocks):
-        store(i).wait()
 
 
 def densify(values, row_ids, col_ids, live_count, row_blocks, col_blocks):
     slots, size, _ = values.shape
-    smem = pl.BlockSpec(memory_space=pltpu.SMEM)
-    hbm = pl.BlockSpec(memory_space=pl.ANY)
+    hbm = pl.BlockSpec(memory_space=pltpu.HBM)
     vmem = pl.BlockSpec(memory_space=pltpu.VMEM)
     rows, cols = row_blocks * size, col_blocks * size
     return pl.pallas_call(
@@ -78,51 +80,47 @@
             jax.ShapeDtypeStruct((rows, cols), jnp.bfloat16),
             jax.ShapeDtypeStruct((row_blocks, 8, size), jnp.float32),
         ),
-        in_specs=[smem, smem, smem, hbm],
-        out_specs=(hbm, vmem),
+        in_specs=[hbm, hbm, hbm, hbm],
+        out_specs=(vmem, vmem),
         scratch_shapes=[
+            pltpu.SMEM((slots,), jnp.int32),
+            pltpu.SMEM((slots,), jnp.int32),
+            pltpu.SMEM((1,), jnp.int32),
             pltpu.VMEM((slots, size, size), jnp.bfloat16),
             pltpu.VMEM((row_blocks, col_blocks, size, size), jnp.float32),
-            pltpu.VMEM((rows, cols), jnp.bfloat16),
             pltpu.SemaphoreType.DMA((4,)),
-            pltpu.SemaphoreType.DMA((row_blocks,)),
+            pltpu.SemaphoreType.DMA((3,)),
         ],
-        compiler_params=pltpu.CompilerParams(vmem_limit_bytes=60 * 1024 * 1024),
+        compiler_params=pltpu.CompilerParams(vmem_limit_bytes=18 * 1024 * 1024),
         name="densify",
     )(row_ids, col_ids, live_count, values)
 
 
 def finish_kernel(
-    own_scale, neigh_scale, g_hbm, out_in, gin_in, bias_in,
-    own_to, neigh_to, out_to, gin_to, bias_to, held, wide, in_sem, out_sem,
+    own_scale, neigh_scale, grads, out_in, gin_in, bias_in,
+    own_to, neigh_to, out_to, gin_to, bias_to, wide, out_sem,
 ):
-    pieces = in_sem.shape[0]
-    rows = g_hbm.shape[1]
+    pieces = out_sem.shape[0]
+    rows = grads.shape[1]
     step = 2 * rows // pieces
-    loads = []
     stores = []
     for p in range(pieces):
         which, at = p % 2, pl.ds(p // 2 * step, step)
         target = (own_to, neigh_to)[which]
-        loads.append(pltpu.make_async_copy(g_hbm.at[which, at], held.at[which, at], in_sem.at[p]))
+        scale = (own_scale, neigh_scale)[which]
+        wide[which, at] = grads[which, at].astype(jnp.float32) * scale
         stores.append(pltpu.make_async_copy(wide.at[which, at], target.at[at], out_sem.at[p]))
-    for load in loads:
-        load.start()
+        stores[p].start()
+    bias_to[...] = bias_in[...] * own_scale
     out_to[...] = out_in[...]
     gin_to[...] = gin_in[...]
-    bias_to[...] = bias_in[...] * own_scale
-    for p in range(pieces):
-        which, at = p % 2, pl.ds(p // 2 * step, step)
-        loads[p].wait()
-        wide[which, at] = held[which, at].astype(jnp.float32) * (own_scale, neigh_scale)[which]
-        stores[p].start()
     for copy in stores:
         copy.wait()
 
 
 def finish(grads, output, grad_input, g_bias, own_scale, neigh_scale):
     _, rows, cols = grads.shape
-    hbm = pl.BlockSpec(memory_space=pl.ANY)
+    hbm = pl.BlockSpec(memory_space=pltpu.HBM)
     vmem = pl.BlockSpec(memory_space=pltpu.VMEM)
     shape = jax.ShapeDtypeStruct
     wide = shape((rows, cols), jnp.float32)
@@ -136,20 +134,19 @@
             shape(grad_input.shape, grad_input.dtype),
             shape(g_bias.shape, g_bias.dtype),
         ),
-        in_specs=[hbm, vmem, vmem, vmem],
+        in_specs=[vmem, vmem, vmem, vmem],
         out_specs=(hbm, hbm, vmem, vmem, vmem),
         scratch_shapes=[
-            pltpu.VMEM((2, rows, cols), jnp.bfloat16),
             pltpu.VMEM((2, rows, cols), jnp.float32),
             pltpu.SemaphoreType.DMA((pieces,)),
-            pltpu.SemaphoreType.DMA((pieces,)),
         ],
-        compiler_params=pltpu.CompilerParams(vmem_limit_bytes=60 * 1024 * 1024),
+        compiler_params=pltpu.CompilerParams(vmem_limit_bytes=24 * 1024 * 1024),
         name="finish",
     )(grads, output, grad_input, g_bias)
 
 
 MESH = pl.DeviceIdType.MESH
+LAYER_VMEM = 36
 BF = jnp.bfloat16
 F32 = jnp.float32
 
@@ -161,9 +158,9 @@
 
 
 def layer_kernel(
-    tile_hbm, mass, features, wn_hbm, ws_hbm, bias, cotangent,
+    tile, mass, features, wn_hbm, ws_hbm, bias, cotangent,
     out_ref, gin_ref, g_ref, gbias_ref,
-    tile, wn, ws, local_sem,
+    wn, ws, local_sem,
     fg, own_feat, send_blocks, recv_blocks, cross_send, cross_recv,
     mass_recv, mass_cross, mass_sum, mixed, group,
     scaled, grounded, sgt, tblock, trecv,
@@ -174,7 +171,7 @@
     gx_s, gx_r, gz_s, gz_r, fw_s, fw_r, pm_s, pm_r, ms_s, ms_r, rs_s, rs_r, rx_s, rx_r,
     sx_s, sx_r, sy_s, sy_r, t_s, t_r,
     ot_s, ot_r, a1_s, a1_r, a2_s, a2_r, a3_s, a3_r, g3_s, g3_r, g2_s, g2_r, g1_s, g1_r, fin_s, fin_r,
-    b_s, b_r, pd_s, pd_r, rz_s, rz_r, rl_s, rl_r, w1_sem, w2_sem,
+    b_s, b_r, pd_s, pd_r, rz_s, rz_r, rl_s, rl_r,
 ):
     r = lax.axis_index("row")
     c = lax.axis_index("col")
@@ -186,7 +183,8 @@
         return (((px % 2) * 4 + pz) * 2 + core, py * 2 + px // 2)
 
     here = (x, y, z)
-    axis_orders = ((0, 1, 2), (1, 2, 0), (2, 0, 1))
+    axis_orders = ((0, 1, 2), (2, 0, 1), (0, 1, 2))
+    gather_orders = ((2, 1, 0), (1, 0, 2), (2, 0, 1))
 
     def along(axis, d):
         spot = list(here)
@@ -211,7 +209,6 @@
         return device[0] * 8 + device[1] == here_id
 
     copies = [
-        pltpu.make_async_copy(tile_hbm, tile, local_sem.at[0]),
         pltpu.make_async_copy(ws_hbm, ws, local_sem.at[1]),
         pltpu.make_async_copy(wn_hbm, wn, local_sem.at[2]),
     ]
@@ -333,7 +330,6 @@
         gather_send(0, 1, d).start()
     spread_gather(1)
 
-    copies[0].wait()
 
     def reduce_send(n, d):
         m = n * 4 + d
@@ -401,8 +397,8 @@
     permute_start(2)
     cross_start(1)
     cross_start(2)
-    copies[1].wait()
-    copies[2].wait()
+    for copy in copies:
+        copy.wait()
 
     for n in range(3):
         permute_wait(n)
@@ -478,26 +474,8 @@
         spread_side(n).start()
         if n == 0:
             spread_more(0, (0,))
-    for n in range(3):
-        part_rows = pl.ds(n * 256, 256)
-        value = lax.dot_general(
-            ws[part_rows, :], grounded[...], turned, preferred_element_type=F32
-        ).astype(BF)
-        for d in range(4):
-            tblock[d, n] = value[d * 64 : (d + 1) * 64]
-
     def self_send(d):
         return remote(tblock.at[d], trecv.at[d], t_s.at[d], t_r.at[d], holder(d))
-
-    for d in range(4):
-
-        @pl.when(jnp.logical_not(is_here(holder(d))))
-        def _():
-            self_send(d).start()
-
-        @pl.when(is_here(holder(d)))
-        def _():
-            trecv[d] = tblock[d]
 
     def self_wait():
         for d in range(4):
@@ -612,15 +590,16 @@
                 halves[n, d, 0, side] = value[:, :128].astype(BF)
                 halves[n, d, 1, side] = value[:, 128:].astype(BF)
             pair_send(n, d).start()
-
-            @pl.when(t > 0)
-            def _():
-                row_send[n, t] = pair_sum(n, t).astype(BF)
-                row_out(n, t).start()
-
             return carry
 
         lax.fori_loop(0, 4, back_step, 0)
+
+        def pair_step(d, carry):
+            row_send[n, d] = pair_sum(n, d).astype(BF)
+            row_out(n, d).start()
+            return carry
+
+        lax.fori_loop(1, 4, pair_step, 0)
         pair_sum(n, 0)
 
     def row_cross(n):
@@ -678,23 +657,28 @@
                 stage3(j, d).start()
         bias_start(2, bias_total(1))
 
-    def place(j, shift, axis_step):
+    def place(j, shift, step):
         a, b, e = axis_orders[j]
+        order = gather_orders[j]
         spot = list(here)
-        moving = axis_orders[j][axis_step]
-        spot[moving] = (spot[moving] + 4 - shift) % 4
-        start = j * 256 + spot[a] * 64
-        if axis_step == 0:
-            return result.at[pl.ds(pl.multiple_of(start, 64), 64)]
-        rows = pl.ds(pl.multiple_of(start + spot[b] * 16, 16), 16)
-        if axis_step == 1:
-            return result.at[rows]
-        return result.at[rows, pl.ds(pl.multiple_of(spot[e] * 256, 256), 256)]
-
-    def back_copy(j, d, axis_step, shift, sends, recvs):
+        spot[order[step]] = (spot[order[step]] + 4 - shift) % 4
+        lead = j * 4 + spot[a]
+        if step == 0:
+            return result.at[lead, spot[b], :, pl.ds(pl.multiple_of(spot[e] * 256, 256), 256)]
+        if step == 1:
+            return result.at[lead, spot[b]]
+        return final(result, j, spot)
+
+    def final(ref, j, spot):
+        a, b, e = axis_orders[j]
+        if gather_orders[j][2] == a:
+            return ref.at[j * 4 + spot[a]]
+        return ref.at[pl.ds(j * 4, 4), spot[b]]
+
+    def back_copy(j, d, step, shift, sends, recvs):
         n = j * 3 + d - 1
-        ref = place(j, shift, axis_step)
-        return remote(ref, ref, sends.at[n], recvs.at[n], along(axis_orders[j][axis_step], d))
+        ref = place(j, shift, step)
+        return remote(ref, ref, sends.at[n], recvs.at[n], along(gather_orders[j][step], d))
 
     def bias_pair(slot):
         return remote(bk.at[slot], bk.at[slot], b_s.at[9], b_r.at[9], partner)
@@ -708,9 +692,9 @@
             total = q2[j, :, cols]
             for d in range(3):
                 total = total + r3[j * 3 + d]
-            place(j, 0, 2)[...] = total.astype(BF)
-            for d in range(1, 4):
-                back_copy(j, d, 2, 0, g3_s, g3_r).start()
+            place(j, 0, 0)[...] = total.astype(BF)
+            for d in range(1, 4):
+                back_copy(j, d, 0, 0, g3_s, g3_r).start()
         bias_core = bias_total(2)
         bk[core] = bias_core
 
@@ -719,7 +703,7 @@
     def ar_gather2():
         for j in range(3):
             for d in range(1, 4):
-                back_copy(j, d, 2, d, g3_s, g3_r).wait_recv()
+                back_copy(j, d, 0, d, g3_s, g3_r).wait_recv()
             for d in range(1, 4):
                 back_copy(j, d, 1, 0, g2_s, g2_r).start()
 
@@ -728,51 +712,131 @@
             for d in range(1, 4):
                 back_copy(j, d, 1, d, g2_s, g2_r).wait_recv()
             for d in range(1, 4):
-                back_copy(j, d, 0, 0, g1_s, g1_r).start()
-
-    def finish_rows(j, d):
-        spot = (here[axis_orders[j][0]] + 4 - d) % 4
-        return pl.ds(pl.multiple_of(j * 256 + spot * 64, 64), 64)
+                back_copy(j, d, 2, 0, g1_s, g1_r).start()
+
+    def last_spot(j, d):
+        axis = gather_orders[j][2]
+        spot = list(here)
+        spot[axis] = (spot[axis] + 4 - d) % 4
+        return spot
 
     def finish_copy(j, d):
         n = j * 4 + d
-        rows = finish_rows(j, d)
-        return remote(result.at[rows], result2.at[rows], fin_s.at[n], fin_r.at[n], partner)
+        spot = last_spot(j, d)
+        return remote(
+            final(result, j, spot), final(result2, j, spot), fin_s.at[n], fin_r.at[n], partner
+        )
 
     def own_out(j, d):
-        ref = result.at[finish_rows(j, d)]
-        return pltpu.make_async_copy(ref, g_ref.at[core, finish_rows(j, d)], w1_sem.at[j * 4 + d])
+        spot = last_spot(j, d)
+        final(g_ref.at[core], j, spot)[...] = final(result, j, spot)[...]
 
     def pair_out(j, d):
-        ref = result2.at[finish_rows(j, d)]
-        return pltpu.make_async_copy(
-            ref, g_ref.at[1 - core, finish_rows(j, d)], w2_sem.at[j * 4 + d]
-        )
+        spot = last_spot(j, d)
+        final(g_ref.at[1 - core], j, spot)[...] = final(result2, j, spot)[...]
 
     def ar_hand():
         for j in range(3):
             finish_copy(j, 0).start()
-            own_out(j, 0).start()
+            own_out(j, 0)
 
     def ar_finish():
         for j in range(3):
             for d in range(1, 4):
-                back_copy(j, d, 0, d, g1_s, g1_r).wait_recv()
+                back_copy(j, d, 2, d, g1_s, g1_r).wait_recv()
                 finish_copy(j, d).start()
-                own_out(j, d).start()
+                own_out(j, d)
         bias_pair(1 - core).wait_recv()
         total = bk[0] + bk[1]
         gbias_ref[...] = jnp.concatenate([total[i : i + 1, :] for i in range(8)], axis=1)
         for j in range(3):
             for d in range(4):
                 finish_copy(j, d).wait_recv()
-                pair_out(j, d).start()
-
+                pair_out(j, d)
+
+    def self_start():
+        for n in range(3):
+            part_rows = pl.ds(n * 256, 256)
+            value = lax.dot_general(
+                ws[part_rows, :], grounded[...], turned, preferred_element_type=F32
+            ).astype(BF)
+            for d in range(4):
+                tblock[d, n] = value[d * 64 : (d + 1) * 64]
+
+        for d in range(4):
+
+            @pl.when(jnp.logical_not(is_here(holder(d))))
+            def _():
+                self_send(d).start()
+
+            @pl.when(is_here(holder(d)))
+            def _():
+                trecv[d] = tblock[d]
+
+    def drain_own():
+        for d in range(4):
+
+            @pl.when(jnp.logical_not(is_here(target(d))))
+            def _():
+                for n in range(3):
+                    permute(n, d).wait_send()
+
+            @pl.when(jnp.logical_not(is_here(holder(d))))
+            def _():
+                self_send(d).wait_send()
+
+    def drain_forward():
+        for n in range(3):
+            side_gather(n).wait_send()
+            cross(n).wait_send()
+            for d in range(1, 4):
+                reduce_send(n, d).wait_send()
+            for s in range(2):
+                for d in range(1, 4):
+                    gather_send(n, s, d).wait_send()
+                for d in range(4):
+                    forward(n, s, d).wait_send()
+        for d in range(1, 4):
+            mass_send(d).wait_send()
+        mass_side().wait_send()
+
+    def drain_back():
+        for n in range(3):
+            spread_side(n).wait_send()
+            row_side(n).wait_send()
+            for d in range(4):
+                pair_send(n, d).wait_send()
+            for d in range(1, 4):
+                row_out(n, d).wait_send()
+                for s in range(2):
+                    spread_send(n, s, d).wait_send()
+
+    def drain_ar():
+        for j in range(3):
+            other_send(j).wait_send()
+            for d in range(1, 4):
+                stage1(j, d).wait_send()
+                stage2(j, d).wait_send()
+                stage3(j, d).wait_send()
+                back_copy(j, d, 0, 0, g3_s, g3_r).wait_send()
+                back_copy(j, d, 1, 0, g2_s, g2_r).wait_send()
+                bias_send(j, d).wait_send()
+
+    def drain_last():
+        for j in range(3):
+            for d in range(1, 4):
+                back_copy(j, d, 2, 0, g1_s, g1_r).wait_send()
+            for d in range(4):
+                finish_copy(j, d).wait_send()
+        bias_pair(core).wait_send()
+
+    self_start()
     spread_more(0, (1,))
     spread_more(1, (0, 1))
     ar_other()
     spread_more(2, (0, 1))
     ar_mine()
+    drain_forward()
     self_wait()
     back(0)
     back(1)
@@ -786,73 +850,19 @@
     ar_gather2()
     ar_gather1()
     ar_hand()
-
-    for n in range(3):
-        row_finish(n)
-    ar_finish()
-
-    for d in range(4):
-
-        @pl.when(jnp.logical_not(is_here(target(d))))
-        def _():
-            for n in range(3):
-                permute(n, d).wait_send()
-
-        @pl.when(jnp.logical_not(is_here(holder(d))))
-        def _():
-            self_send(d).wait_send()
-
-    def drain_forward():
-        for n in range(3):
-            side_gather(n).wait_send()
-            cross(n).wait_send()
-            for d in range(1, 4):
-                reduce_send(n, d).wait_send()
-            for s in range(2):
-                for d in range(1, 4):
-                    gather_send(n, s, d).wait_send()
-                for d in range(4):
-                    forward(n, s, d).wait_send()
-        for d in range(1, 4):
-            mass_send(d).wait_send()
-        mass_side().wait_send()
-
-    def drain_back():
-        for n in range(3):
-            spread_side(n).wait_send()
-            row_side(n).wait_send()
-            for d in range(4):
-                pair_send(n, d).wait_send()
-            for d in range(1, 4):
-                row_out(n, d).wait_send()
-                for s in range(2):
-                    spread_send(n, s, d).wait_send()
-
-    def drain_ar():
-        for j in range(3):
-            other_send(j).wait_send()
-            for d in range(1, 4):
-                stage1(j, d).wait_send()
-                stage2(j, d).wait_send()
-                stage3(j, d).wait_send()
-                back_copy(j, d, 2, 0, g3_s, g3_r).wait_send()
-                back_copy(j, d, 1, 0, g2_s, g2_r).wait_send()
-                back_copy(j, d, 0, 0, g1_s, g1_r).wait_send()
-                bias_send(j, d).wait_send()
-            for d in range(4):
-                finish_copy(j, d).wait_send()
-                own_out(j, d).wait()
-                pair_out(j, d).wait()
-        bias_pair(core).wait_send()
-
-    drain_forward()
+    row_finish(0)
+    row_finish(1)
+    row_finish(2)
+    drain_own()
     drain_back()
     drain_ar()
+    ar_finish()
+    drain_last()
 
 
 def layer(tile, mass, features, w_neigh, w_self, bias, cotangent):
     vmem = pl.BlockSpec(memory_space=pltpu.VMEM)
-    hbm = pl.BlockSpec(memory_space=pl.ANY)
+    hbm = pl.BlockSpec(memory_space=pltpu.HBM)
     sem = pltpu.SemaphoreType.DMA
     V = pltpu.VMEM
     shape = jax.ShapeDtypeStruct
@@ -861,13 +871,13 @@
         out_shape=(
             shape((128, 1024), BF),
             shape((128, 768), BF),
-            shape((2, 768, 1024), BF),
+            shape((2, 12, 4, 16, 1024), BF),
             shape((1, 1024), F32),
         ),
-        in_specs=[hbm, vmem, vmem, hbm, hbm, vmem, vmem],
-        out_specs=(vmem, vmem, hbm, vmem),
+        in_specs=[vmem, vmem, vmem, hbm, hbm, vmem, vmem],
+        out_specs=(vmem, vmem, vmem, vmem),
         scratch_shapes=[
-            V((1024, 2048), BF), V((768, 1024), BF), V((768, 1024), BF), sem((3,)),
+            V((768, 1024), BF), V((768, 1024), BF), sem((3,)),
             V((3, 2048, 256), BF), V((3, 128, 256), BF), V((3, 4, 256, 256), BF),
             V((3, 3, 256, 256), BF), V((3, 128, 256), BF), V((3, 128, 256), BF),
             V((3, 2, 8, 128), F32), V((8, 128), F32), V((2, 8, 128), F32), V((128, 768), F32),
@@ -876,7 +886,7 @@
             V((128, 768), BF), V((128, 1024), BF), V((128, 768), BF), V((128, 1024), BF),
             V((768, 1024), BF), V((768, 1024), BF), V((768, 1024), BF),
             V((9, 64, 1024), BF), V((3, 64, 1024), F32), V((9, 16, 1024), F32), V((3, 16, 1024), F32),
-            V((9, 16, 256), F32), V((768, 1024), BF), V((768, 1024), BF),
+            V((9, 16, 256), F32), V((12, 4, 16, 1024), BF), V((12, 4, 16, 1024), BF),
             V((3, 4, 2, 2, 256, 128), BF), V((3, 4, 2, 256, 128), BF), V((3, 4, 2, 256, 128), BF),
             V((3, 3, 2, 256, 128), BF), V((3, 2, 256, 128), F32), V((3, 256, 128), BF), V((3, 256, 128), BF),
             V((1, 1024), F32), V((4, 8, 128), F32), V((4, 8, 128), F32), V((4, 8, 128), F32), V((2, 8, 128), F32),
@@ -884,9 +894,9 @@
         + [sem((3,))] * 2 + [sem((24,))] * 4 + [sem((12,))] * 2 + [sem((4,))] * 2 + [sem((12,))] * 2
         + [sem((3,))] * 4 + [sem((24,))] * 2 + [sem((4,))] * 2 + [sem((3,))] * 2
         + [sem((9,))] * 12 + [sem((12,))] * 2 + [sem((10,))] * 2 + [sem((12,))] * 4 + [sem((3,))] * 2
-        + [sem((12,))] * 2,
+        ,
         compiler_params=pltpu.CompilerParams(
-            collective_id=0, has_side_effects=True, vmem_limit_bytes=58 * 1024 * 1024
+            collective_id=0, has_side_effects=True, vmem_limit_bytes=LAYER_VMEM * 1024 * 1024
         ),
         name="layer",
     )(tile, mass, features, w_neigh, w_self, bias, cotangent)
@@ -906,7 +916,7 @@
     )
     factor = 1.0 / math.sqrt(node_dev * row_size * col_size)
     grad_self, grad_neigh, output, grad_input, g_bias = finish(
-        grads, output, grad_input, g_bias, factor, 32.0 * factor
+        grads.reshape(2, 768, 1024), output, grad_input, g_bias, factor, 32.0 * factor
     )
     return output, grad_input, grad_self, grad_neigh, g_bias.reshape(-1)
 

time: 133 us -> 129 us (0.970)
  Pallas kernels: 131 us -> 122 us
  local copies, waits for them, and re-layouts: 0 us -> 5.08 us
    unnamed x0 -> x16, local copies, waits for them, and re-layouts: none -> 5.08 us
    pallas_call x1, Pallas kernels: 120 us -> 115 us  [layer(): pl.pallas_call(layer_kernel, out_shape=(shape((128, 1024), BF), shape((12...]
    pallas_call x1, Pallas kernels: 5.55 us -> 3.19 us  [densify(): pl.pallas_call(densify_kernel, out_shape=(jax.ShapeDtypeStruct((rows, col...]
    pallas_call x1, Pallas kernels: 5.67 us -> 3.56 us  [finish(): pl.pallas_call(functools.partial(finish_kernel, own_scale, neigh_scale),...]
where the time goes in v4:
time: 129 us; the launch traced here: 128 us
  Pallas kernels  122 us (95%)
  local copies, waits for them, and re-layouts  5.08 us (4%)
  between operations  1.36 us (1%)
    pallas_call x1, Pallas kernels, layer(): pl.pallas_call(layer_kernel, out_shape=(shape((128, 1024), BF), shape((12...  115 us
    unnamed x16, local copies, waits for them, and re-layouts  5.08 us
    pallas_call x1, Pallas kernels, finish(): pl.pallas_call(functools.partial(finish_kernel, own_scale, neigh_scale),...  3.56 us
    pallas_call x1, Pallas kernels, densify(): pl.pallas_call(densify_kernel, out_shape=(jax.ShapeDtypeStruct((rows, col...  3.19 us

profile of v4, /device:TPU:1, one launch (start us, length us, event | category | flops | bytes accessed | tf_op | source)
XLA Modules:
  0.0 128.4 jit_solution(8388622548881959619)
XLA Ops:
  0.6 0.0 copy-start.5
  1.3 0.0 copy-start
  1.3 1.9 %copy-done = bf16[1,1,96,128,128]{4,3,2,1,0:T(8,128)(2,1)S(1)} copy-done((bf16[1,1,96,128,128]{4,3,2,1,0:T(8,128)(2,1)S(1)}, bf16[1,1,96,128,128]{4,3,2,1,0:T(8,128)(2,1)}, u32[]{:S(2)}) %copy-start) | copy-done | bytes 3145752
  3.2 0.0 copy-start.6
  3.2 0.7 copy-done.6
  3.8 0.0 copy-start.7
  3.9 0.7 copy-done.7
  4.5 0.0 copy-start.1
  4.5 0.0 copy-start.2
  4.5 3.2 %densify.1 = (bf16[1024,2048]{1,0:T(8,128)(2,1)S(1)}, f32[8,8,128]{2,1,0:T(8,128)S(1)}) custom-call(s32[96]{0:T(128)S(1)} %bitcast.11, s32[96]{0:T(128)S(1)} %bitcast.12, s32[1]{0:T(128)} %bitcast.7.count_hbm, bf16[96,128,128]{2,1,0:T(8,128)(2,1)S(1)} %bitcast.8), custom_call_target="tpu_custom_call" | custom-call | tf_op jit(solution)/shard_map/densify/pallas_call | solution.py:77
  7.7 0.0 copy-done.5
  7.7 0.0 copy-done.1
  7.7 0.0 copy-done.2
  7.7 0.0 copy-start.3
  7.7 0.9 copy-done.3
  8.7 0.0 copy-start.4
  8.7 0.9 copy-done.4
  9.6 115.2 %layer.1 = (bf16[128,1024]{1,0:T(8,128)(2,1)S(1)}, bf16[128,768]{1,0:T(8,128)(2,1)S(1)}, bf16[2,12,4,16,1024]{4,3,2,1,0:T(8,128)(2,1)S(1)}, f32[1,1024]{1,0:T(1,128)S(1)}) custom-call(bf16[1024,2048]{1,0:T(8,128)(2,1)S(1)} %get-tuple-element.16.tile, f32[8,8,128]{2,1,0:T(8,128)S(1)} %get-tuple-element.17.mass, bf16[128,768]{1,0:T(8,128)(2,1)S(1)} %copy-done.4, ...), custom_call_target="tpu_custom_call" | custom-call | tf_op jit(solution)/shard_map/layer/pallas_call | solution.py:869
  124.8 3.6 %finish.1 = (f32[768,1024]{1,0:T(8,128)}, f32[768,1024]{1,0:T(8,128)}, bf16[128,1024]{1,0:T(8,128)(2,1)}, bf16[128,768]{1,0:T(8,128)(2,1)}, f32[1,1024]{1,0:T(1,128)}) custom-call(bf16[2,768,1024]{2,1,0:T(8,128)(2,1)S(1)} %bitcast.9, bf16[128,1024]{1,0:T(8,128)(2,1)S(1)} %get-tuple-element.19.out_in, bf16[128,768]{1,0:T(8,128)(2,1)S(1)} %get-tuple-element.20.gin_in, ...), custom_call_target="tpu_custom_call" | custom-call | tf_op jit(solution)/shard_map/finish/pallas_call | solution.py:128
Async XLA Ops:
  0.6 7.1 %copy-start.5 = (f32[1024]{0:T(1024)S(1)}, f32[1024]{0:T(1024)}, u32[]{:S(2)}) copy-start(f32[1024]{0:T(1024)} %param.12) | copy-start | bytes 12292
  1.3 1.9 %copy-start = (bf16[1,1,96,128,128]{4,3,2,1,0:T(8,128)(2,1)S(1)}, bf16[1,1,96,128,128]{4,3,2,1,0:T(8,128)(2,1)}, u32[]{:S(2)}) copy-start(bf16[1,1,96,128,128]{4,3,2,1,0:T(8,128)(2,1)} %param.16) | copy-start | bytes 9437188
  3.2 0.7 copy-start.6
  3.8 0.7 copy-start.7
  4.5 3.2 %copy-start.1 = (bf16[768,1024]{1,0:T(8,128)(2,1)S(1)}, bf16[768,1024]{1,0:T(8,128)(2,1)}, u32[]{:S(2)}) copy-start(bf16[768,1024]{1,0:T(8,128)(2,1)} %wn_hbm.1) | copy-start | bytes 4718596
  4.5 3.2 %copy-start.2 = (bf16[768,1024]{1,0:T(8,128)(2,1)S(1)}, bf16[768,1024]{1,0:T(8,128)(2,1)}, u32[]{:S(2)}) copy-start(bf16[768,1024]{1,0:T(8,128)(2,1)} %ws_hbm.1) | copy-start | bytes 4718596
  7.7 1.0 copy-start.3
  8.7 0.9 copy-start.4

commit v5 on v4

--- a/solution.py
+++ b/solution.py
@@ -384,9 +384,7 @@
         cross(n).start()
 
     mix(0)
-    permute_start(0)
     mix(1)
-    permute_start(1)
     cross_start(0)
     for d in range(1, 4):
         mass_send(d).wait_recv()
@@ -394,6 +392,8 @@
         mass_sum[h] = mass[y * 2 + h] + ((mass_recv[0, h] + mass_recv[1, h]) + mass_recv[2, h])
     mass_side().start()
     mix(2)
+    permute_start(0)
+    permute_start(1)
     permute_start(2)
     cross_start(1)
     cross_start(2)

time: 129 us -> 129 us (level)
  no operation moved by 1% of the time
where the time goes in v5:
time: 129 us
  Pallas kernels  123 us (95%)
  local copies, waits for them, and re-layouts  5.08 us (4%)
  between operations  1.36 us (1%)
    pallas_call x1, Pallas kernels, layer(): pl.pallas_call(layer_kernel, out_shape=(shape((128, 1024), BF), shape((12...  116 us
    unnamed x16, local copies, waits for them, and re-layouts  5.08 us
    pallas_call x1, Pallas kernels, finish(): pl.pallas_call(functools.partial(finish_kernel, own_scale, neigh_scale),...  3.56 us
    pallas_call x1, Pallas kernels, densify(): pl.pallas_call(densify_kernel, out_shape=(jax.ShapeDtypeStruct((rows, col...  3.11 us

profile of v5, /device:TPU:1, one launch (start us, length us, event | category | flops | bytes accessed | tf_op | source)
XLA Modules:
  0.0 129.1 jit_solution(1307432008656529570)
XLA Ops:
  0.6 0.0 copy-start.5
  1.3 0.0 copy-start
  1.3 1.9 %copy-done = bf16[1,1,96,128,128]{4,3,2,1,0:T(8,128)(2,1)S(1)} copy-done((bf16[1,1,96,128,128]{4,3,2,1,0:T(8,128)(2,1)S(1)}, bf16[1,1,96,128,128]{4,3,2,1,0:T(8,128)(2,1)}, u32[]{:S(2)}) %copy-start) | copy-done | bytes 3145752
  3.2 0.0 copy-start.6
  3.2 0.7 copy-done.6
  3.8 0.0 copy-start.7
  3.9 0.7 copy-done.7
  4.5 0.0 copy-start.1
  4.5 0.0 copy-start.2
  4.5 3.1 %densify.1 = (bf16[1024,2048]{1,0:T(8,128)(2,1)S(1)}, f32[8,8,128]{2,1,0:T(8,128)S(1)}) custom-call(s32[96]{0:T(128)S(1)} %bitcast.11, s32[96]{0:T(128)S(1)} %bitcast.12, s32[1]{0:T(128)} %bitcast.7.count_hbm, bf16[96,128,128]{2,1,0:T(8,128)(2,1)S(1)} %bitcast.8), custom_call_target="tpu_custom_call" | custom-call | tf_op jit(solution)/shard_map/densify/pallas_call | solution.py:77
  7.6 0.0 copy-done.5
  7.6 0.0 copy-done.1
  7.6 0.0 copy-done.2
  7.7 0.0 copy-start.3
  7.7 0.9 copy-done.3
  8.6 0.0 copy-start.4
  8.6 0.9 copy-done.4
  9.5 116.0 %layer.1 = (bf16[128,1024]{1,0:T(8,128)(2,1)S(1)}, bf16[128,768]{1,0:T(8,128)(2,1)S(1)}, bf16[2,12,4,16,1024]{4,3,2,1,0:T(8,128)(2,1)S(1)}, f32[1,1024]{1,0:T(1,128)S(1)}) custom-call(bf16[1024,2048]{1,0:T(8,128)(2,1)S(1)} %get-tuple-element.16.tile, f32[8,8,128]{2,1,0:T(8,128)S(1)} %get-tuple-element.17.mass, bf16[128,768]{1,0:T(8,128)(2,1)S(1)} %copy-done.4, ...), custom_call_target="tpu_custom_call" | custom-call | tf_op jit(solution)/shard_map/layer/pallas_call | solution.py:869
  125.5 3.6 %finish.1 = (f32[768,1024]{1,0:T(8,128)}, f32[768,1024]{1,0:T(8,128)}, bf16[128,1024]{1,0:T(8,128)(2,1)}, bf16[128,768]{1,0:T(8,128)(2,1)}, f32[1,1024]{1,0:T(1,128)}) custom-call(bf16[2,768,1024]{2,1,0:T(8,128)(2,1)S(1)} %bitcast.9, bf16[128,1024]{1,0:T(8,128)(2,1)S(1)} %get-tuple-element.19.out_in, bf16[128,768]{1,0:T(8,128)(2,1)S(1)} %get-tuple-element.20.gin_in, ...), custom_call_target="tpu_custom_call" | custom-call | tf_op jit(solution)/shard_map/finish/pallas_call | solution.py:128
Async XLA Ops:
  0.6 7.0 %copy-start.5 = (f32[1024]{0:T(1024)S(1)}, f32[1024]{0:T(1024)}, u32[]{:S(2)}) copy-start(f32[1024]{0:T(1024)} %param.12) | copy-start | bytes 12292
  1.3 1.9 %copy-start = (bf16[1,1,96,128,128]{4,3,2,1,0:T(8,128)(2,1)S(1)}, bf16[1,1,96,128,128]{4,3,2,1,0:T(8,128)(2,1)}, u32[]{:S(2)}) copy-start(bf16[1,1,96,128,128]{4,3,2,1,0:T(8,128)(2,1)} %param.16) | copy-start | bytes 9437188
  3.2 0.7 copy-start.6
  3.8 0.7 copy-start.7
  4.5 3.1 %copy-start.1 = (bf16[768,1024]{1,0:T(8,128)(2,1)S(1)}, bf16[768,1024]{1,0:T(8,128)(2,1)}, u32[]{:S(2)}) copy-start(bf16[768,1024]{1,0:T(8,128)(2,1)} %wn_hbm.1) | copy-start | bytes 4718596
  4.5 3.1 %copy-start.2 = (bf16[768,1024]{1,0:T(8,128)(2,1)S(1)}, bf16[768,1024]{1,0:T(8,128)(2,1)}, u32[]{:S(2)}) copy-start(bf16[768,1024]{1,0:T(8,128)(2,1)} %ws_hbm.1) | copy-start | bytes 4718596
  7.7 1.0 copy-start.3
  8.6 0.9 copy-start.4
